TPU v7x, 512 devices: a whole 4x8x8 slice. The times are simulated.
512 devices in a mesh: ctx: 64 (over y, z), head: 4 (over x), row: 2 (over core).
Axes of the slice: x: 4, y: 8, z: 8, core: 2. Of those that a mesh axis runs over, the one named last changes fastest.
Arguments:
- hidden_states: bfloat16 [32768, 3584], P(('row', 'ctx'), 'head'), parts along dimension 0, may hold values from -40 to 40
- w_query: bfloat16 [3584, 3584], P('ctx', 'head'), may hold values from -0.09375 to 0.09375
- key_weight_matrix: bfloat16 [3584, 512], P('ctx', 'head'), may hold values from -0.09375 to 0.09375
- value_weight_matrix: bfloat16 [3584, 512], P('ctx', 'head'), may hold values from -0.09375 to 0.09375
- bias_query: float32 [3584], P('head'), may hold values from -40 to 40
- bias_key: float32 [512], P('head'), may hold values from -40 to 40
- value_bias_vector: float32 [512], P('head'), may hold values from -5 to 5
- published: int32 [128, 4], P(('row', 'ctx'), 'head'), parts along dimension 0, may hold values from 0 to 1
- vertical: int32 [128, 4, 8], P(('row', 'ctx'), 'head'), parts along dimension 0, may hold values from 0 to 62, as said below
- vcount: int32 [128, 4], P(('row', 'ctx'), 'head'), parts along dimension 0, may hold values from 0 to 8, as said below
- slash_offsets: int32 [128, 4, 16], P(('row', 'ctx'), 'head'), parts along dimension 0, may hold values from 0 to 256, as said below
- scount: int32 [128, 4], P(('row', 'ctx'), 'head'), parts along dimension 0, may hold values from 1 to 16
Outputs:
- attention: bfloat16 [32768, 3584], P(('row', 'ctx'), 'head'), parts along dimension 0
There are 2 independent parts, one for each index of `row`. A program takes and returns all parts, laid end to end along the dimension named above; an argument that names none is the same for every part. Nothing has to cross between parts.
Inputs may be any that keep to these rules, and one draw needn't show every extreme that they name: `vertical`: for span c and head g the first vcount[c, g] entries are distinct span numbers of at most c - 1; the remaining entries are 0. vcount[c, g] is at most min(8, c); the last span's lists are full. `slash_offsets`: for span c and head g the first scount[c, g] entries are distinct; the remaining entries are 0.
All inputs are finite; a program needn't handle non-finite values.
Results may differ from a plain program's by a relative error of at most 0.007.
The roundings to bfloat16 on the way count: a program that leaves them out, or rounds other values in their place, can miss the bound.
Values may be sent and summed in bfloat16 or wider, within the bound.
A program may use at most 64 MiB of HBM per device.

v0:
```python
import jax
import jax.numpy as jnp
from jax import lax
from jax.sharding import PartitionSpec as P

KEY_BLOCK_TOKENS = 128


def from_behind(block, axis, distance):
    devices = range(lax.axis_size(axis))
    route = [(i - distance, i) for i in devices if i - distance in devices]
    return lax.ppermute(block, axis, route)


def frequencies(head_width):
    exponents = jnp.arange(0, head_width, 2).astype(jnp.float32) / head_width
    return jnp.power(jnp.float32(10000000.0), -exponents)


def rotate(inputs, angles):
    half_width = inputs.shape[-1] // 2
    first_half = inputs[..., :half_width]
    second_half = inputs[..., half_width:]
    cosine = jnp.cos(angles)
    sine_part = jnp.sin(angles)
    return jnp.concatenate(
        [
            first_half * cosine - second_half * sine_part,
            second_half * cosine + first_half * sine_part,
        ],
        axis=-1,
    )


def on_device(
    hidden_states,
    w_query,
    key_weight_matrix,
    value_weight_matrix,
    bias_query,
    bias_key,
    value_bias_vector,
    published,
    vertical,
    vcount,
    slash_offsets,
    scount,
):
    tok_count = hidden_states.shape[0]
    head_width = bias_key.shape[0]
    group_size = bias_query.shape[0] // head_width
    score_scale = head_width ** (-0.5)
    gathered = lax.all_gather(hidden_states, "head", axis=1, tiled=True)
    weights_all = (
        lax.all_gather(w_query, "ctx", axis=0, tiled=True),
        lax.all_gather(key_weight_matrix, "ctx", axis=0, tiled=True),
        lax.all_gather(value_weight_matrix, "ctx", axis=0, tiled=True),
    )
    query_rows = jnp.dot(gathered, weights_all[0], preferred_element_type=jnp.float32)
    unrotated_keys = jnp.dot(gathered, weights_all[1], preferred_element_type=jnp.float32)
    values_raw = jnp.dot(gathered, weights_all[2], preferred_element_type=jnp.float32)
    query_rows = (query_rows + bias_query).reshape(tok_count, group_size, head_width)
    unrotated_keys = unrotated_keys + bias_key
    every_value_row = (values_raw + value_bias_vector).astype(jnp.bfloat16)
    inverse = frequencies(head_width)
    positions = jnp.arange(tok_count).astype(jnp.float32)
    angle_local = positions[:, None] * inverse[None, :]
    angle_near = (positions + tok_count)[:, None] * inverse[None, :]
    angle_far = jnp.full((1,), 2 * tok_count - 1).astype(jnp.float32)[:, None] * inverse[None, :]
    rotary_keys = rotate(unrotated_keys, angle_local).astype(jnp.bfloat16)
    query_local = rotate(query_rows, angle_local[:, None, :]).astype(jnp.bfloat16)
    query_near = rotate(query_rows, angle_near[:, None, :]).astype(jnp.bfloat16)
    query_far = rotate(query_rows, angle_far[:, None, :]).astype(jnp.bfloat16)
    prior_key, prior_value = from_behind((rotary_keys, every_value_row), "ctx", 1)
    span_index = lax.axis_index("ctx")
    block_start = published[0, 0] * KEY_BLOCK_TOKENS
    own_key = lax.dynamic_slice_in_dim(rotary_keys, block_start, KEY_BLOCK_TOKENS, 0)[None]
    own_value = lax.dynamic_slice_in_dim(every_value_row, block_start, KEY_BLOCK_TOKENS, 0)[None]
    pooled_keys, pooled_values = (
        lax.all_gather(own_key, "ctx", axis=0, tiled=True),
        lax.all_gather(own_value, "ctx", axis=0, tiled=True),
    )
    chosen_columns = vertical[0, 0]
    list_slots = chosen_columns.shape[0]
    far_key = jnp.take(pooled_keys, chosen_columns, axis=0).reshape(
        list_slots * KEY_BLOCK_TOKENS, head_width
    )
    far_value = jnp.take(pooled_values, chosen_columns, axis=0).reshape(
        list_slots * KEY_BLOCK_TOKENS, head_width
    )
    live_far = jnp.repeat(jnp.arange(list_slots) < vcount[0, 0], KEY_BLOCK_TOKENS)
    offsets = slash_offsets[0, 0]
    slash_slots = offsets.shape[0]
    places = jnp.arange(tok_count)[:, None]
    valid_near = (
        (offsets[None, :] > places)
        & (jnp.arange(slash_slots) < scount[0, 0])[None, :]
        & (span_index > 0)
    )
    slash_index = jnp.where(valid_near, places - offsets[None, :] + tok_count, 0)
    near_key = prior_key[slash_index]
    near_value = prior_value[slash_index]
    causal = jnp.arange(tok_count)[:, None] >= jnp.arange(tok_count)[None, :]

    def one_head(inputs):
        local_q, near_q, far_q = inputs
        score_local = (
            jnp.einsum("td,jd->tj", local_q, rotary_keys, preferred_element_type=jnp.float32)
            * score_scale
        )
        score_local = jnp.where(causal, score_local, -jnp.inf)
        score_far = (
            jnp.einsum("td,kd->tk", far_q, far_key, preferred_element_type=jnp.float32)
            * score_scale
        )
        score_far = jnp.where(live_far[None, :], score_far, -jnp.inf)
        score_near = (
            jnp.einsum("td,tnd->tn", near_q, near_key, preferred_element_type=jnp.float32)
            * score_scale
        )
        score_near = jnp.where(valid_near, score_near, -jnp.inf)
        highest = jnp.maximum(
            jnp.max(score_local, axis=-1, keepdims=True),
            jnp.maximum(
                jnp.max(score_far, axis=-1, keepdims=True),
                jnp.max(score_near, axis=-1, keepdims=True),
            ),
        )
        expo_local = jnp.exp(score_local - highest)
        expo_far = jnp.exp(score_far - highest)
        expo_near = jnp.exp(score_near - highest)
        totals = (
            jnp.sum(expo_local, axis=-1, keepdims=True)
            + jnp.sum(expo_far, axis=-1, keepdims=True)
            + jnp.sum(expo_near, axis=-1, keepdims=True)
        )
        weight_local = (expo_local / totals).astype(jnp.bfloat16)
        weight_far = (expo_far / totals).astype(jnp.bfloat16)
        weight_near = (expo_near / totals).astype(jnp.bfloat16)
        combined = jnp.dot(weight_local, every_value_row, preferred_element_type=jnp.float32)
        combined = combined + jnp.dot(weight_far, far_value, preferred_element_type=jnp.float32)
        combined = combined + jnp.einsum(
            "tn,tnd->td", weight_near, near_value, preferred_element_type=jnp.float32
        )
        return combined.astype(jnp.bfloat16)

    per_head = lax.map(
        one_head,
        (
            query_local.transpose(1, 0, 2),
            query_near.transpose(1, 0, 2),
            query_far.transpose(1, 0, 2),
        ),
    )
    return per_head.transpose(1, 0, 2).reshape(tok_count, group_size * head_width)


def solution(mesh):
    in_specs = (
        P(("row", "ctx"), "head"),
        P("ctx", "head"),
        P("ctx", "head"),
        P("ctx", "head"),
        P("head"),
        P("head"),
        P("head"),
        P(("row", "ctx"), "head"),
        P(("row", "ctx"), "head", None),
        P(("row", "ctx"), "head"),
        P(("row", "ctx"), "head", None),
        P(("row", "ctx"), "head"),
    )
    out_specs = P(("row", "ctx"), "head")
    return jax.shard_map(
        on_device, mesh=mesh, in_specs=in_specs, out_specs=out_specs, check_vma=False
    )
```

profile of v0, /device:TPU:6, one launch (start us, length us, event | category | flops | bytes accessed | tf_op | source)
XLA Modules:
  0.0 391.5 jit_solution(5671231126623350382)
XLA Ops:
  8.0 57.6 %all_gather.20 = bf16[3584,128]{1,0:T(8,128)(2,1)S(1)} all-gather(bf16[56,128]{1,0:T(8,128)(2,1)} %param.18), channel_id=1, replica_groups=mesh['ctx'=64,'head'=4,'row'=2] {'ctx'}, dimensions={0}, use_global_device_ids=true | all-gather | bytes 931840 | tf_op jit(solution)/shard_map/all_gather | solution.py:56
  65.7 2.4 convolution_add_fusion.3
  70.0 48.6 %all_gather.22 = bf16[3584,128]{1,0:T(8,128)(2,1)S(1)} all-gather(bf16[56,128]{1,0:T(8,128)(2,1)S(1)} %copy-done.8), channel_id=1, replica_groups=mesh['ctx'=64,'head'=4,'row'=2] {'ctx'}, dimensions={0}, use_global_device_ids=true | all-gather | bytes 931840 | tf_op jit(solution)/shard_map/all_gather | solution.py:57
  122.1 2.3 collective-permute-start.1
  124.5 2.5 collective-permute-start
  127.6 1.7 collective-permute-done
  129.4 14.9 %gather_fusion = bf16[4096,128]{1,0:T(8,128)(2,1)} fusion(bf16[256,128]{1,0:T(8,128)(2,1)S(1)} %copy.34, s32[4096]{0:T(1024)S(1)} %broadcast_clamp_fusion), kind=kCustom, calls=%fused_computation.2 | custom fusion | bytes 2113536 | tf_op jit(solution)/shard_map/gather | solution.py:101
  144.3 14.9 %gather_fusion.1 = bf16[4096,128]{1,0:T(8,128)(2,1)} fusion(bf16[256,128]{1,0:T(8,128)(2,1)S(1)} %collective-permute-done.1, s32[4096]{0:T(1024)S(1)} %broadcast_clamp_fusion), kind=kCustom, calls=%fused_computation.3 | custom fusion | bytes 2113536 | tf_op jit(solution)/shard_map/gather | solution.py:102
  159.2 4.1 %copy.45 = bf16[8192,128]{1,0:T(8,128)(2,1)} copy(bf16[8192,128]{0,1:T(8,128)(2,1)} %all-gather.11.cloned.1.call-done) | data formatting | bytes 4194304 | tf_op jit(solution)/shard_map/all_gather | solution.py:80
  163.3 2.2 gather_fusion.2
  165.5 66.8 %all-gather.13.cloned.1.call-done = bf16[8192,128]{1,0:T(8,128)(2,1)} async-done(((bf16[128,128]{1,0:T(8,128)(2,1)}), bf16[8192,128]{1,0:T(8,128)(2,1)}) %all-gather.13.cloned.1.call-update) | async-done | bytes 2097168 | tf_op jit(solution)/shard_map/all_gather | solution.py:81
  232.2 2.2 gather_fusion.3
  235.2 88.1 %all-gather.9.cloned.1.call-done = bf16[3584,896]{1,0:T(8,128)(2,1)} async-done(((bf16[56,896]{1,0:T(8,128)(2,1)}), bf16[3584,896]{1,0:T(8,128)(2,1)}) %all-gather.9.cloned.1.call-update) | async-done | bytes 6422544 | tf_op jit(solution)/shard_map/all_gather | solution.py:55
  323.3 4.9 %convolution_add_fusion.1 = f32[256,896]{1,0:T(8,128)S(1)} fusion(bf16[256,3584]{1,0:T(8,128)(2,1)S(1)} %copy-done, bf16[3584,896]{1,0:T(8,128)(2,1)} %all-gather.9.cloned.1.call-done, f32[896]{0:T(1024)} %param.20), kind=kOutput, calls=%fused_computation.46 | convolution fusion | flops 1644396544 | bytes 9178624 | tf_op jit(solution)/shard_map/dot_general | solution.py:59
  330.4 53.6 %while.11 = (s32[]{:T(128)}, bf16[7,256,128]{1,2,0:T(8,128)(2,1)S(1)}, bf16[7,256,128]{1,2,0:T(8,128)(2,1)S(1)}, bf16[256,128]{1,0:T(8,128)(2,1)S(1)}, bf16[7,25...) while((s32[]{:T(128)}, ...), condition=%wide.region_7.9_spmd.clone, body=%wide.region_0.8_spmd.clone.sunk | while | flops 172740096 | bytes 8152488 | solution.py:147
  330.6 1.9 fusion.77
  338.3 1.9 fusion.77
  345.9 1.9 fusion.77
  350.2 1.6 fusion.83
  353.6 1.9 fusion.77
  357.9 1.6 fusion.83
  361.2 1.9 fusion.77
  368.9 1.9 fusion.77
  376.5 1.9 fusion.77
  (193 shorter events, 46.2 us)
Async XLA Ops:
  6.5 59.1 %all-gather.7.cloned.1.call-start = ((), (), s32[]{:S(2)}) async-start(), calls=%async_computation | async-start | bytes 2293760 | tf_op jit(solution)/shard_map/all_gather | solution.py:53
  7.3 151.9 %all-gather.11.cloned.1.call-start = ((), (), s32[]{:S(2)}) async-start(), calls=%async_computation.2 | async-start | bytes 2129920 | tf_op jit(solution)/shard_map/all_gather | solution.py:80
  65.6 4.3 %copy-start.8 = (bf16[56,128]{1,0:T(8,128)(2,1)S(1)}, bf16[56,128]{1,0:T(8,128)(2,1)}, u32[]{:S(2)}) copy-start(bf16[56,128]{1,0:T(8,128)(2,1)} %param.19) | copy-start | bytes 43012
  65.6 52.9 %copy-start.9 = (f32[128]{0:T(128)S(1)}, f32[128]{0:T(128)}, u32[]{:S(2)}) copy-start(f32[128]{0:T(128)} %param.22) | copy-start | bytes 1540
  65.7 52.9 %copy-start = (bf16[256,3584]{1,0:T(8,128)(2,1)S(1)}, bf16[256,3584]{1,0:T(8,128)(2,1)}, u32[]{:S(2)}) copy-start(bf16[256,3584]{1,0:T(8,128)(2,1)} %all-gather.7.cloned.1.call-done) | copy-start | bytes 5505028
  69.9 51.9 %copy-start.7 = (s32[1,1,16]{2,1,0:T(1,128)S(1)}, s32[1,1,16]{2,1,0:T(1,128)}, u32[]{:S(2)}) copy-start(s32[1,1,16]{2,1,0:T(1,128)} %param.26) | copy-start | bytes 196
  69.9 162.3 %all-gather.13.cloned.1.call-start = ((), (), s32[]{:S(2)}) async-start(), calls=%async_computation.3 | async-start | bytes 2129920 | tf_op jit(solution)/shard_map/all_gather | solution.py:81
  118.6 3.5 copy-start.10
  119.2 25.1 %copy-start.5 = (bf16[256,128]{1,0:T(8,128)(2,1)}, bf16[256,128]{1,0:T(8,128)(2,1)S(1)}, u32[]{:S(2)}) copy-start(bf16[256,128]{1,0:T(8,128)(2,1)S(1)} %fusion.28) | copy-start | bytes 196612
  119.9 203.5 %all-gather.9.cloned.1.call-start = ((), (), s32[]{:S(2)}) async-start(), calls=%async_computation.1 | async-start | bytes 6522880 | tf_op jit(solution)/shard_map/all_gather | solution.py:55
  122.1 22.2 %collective-permute-start.1 = (bf16[256,128]{1,0:T(8,128)(2,1)S(1)}, bf16[256,128]{1,0:T(8,128)(2,1)S(1)}, u32[]{:S(2)}, u32[]{:S(2)}) collective-permute-start(bf16[256,128]{1,0:T(8,128)(2,1)S(1)} %fusion.28), channel_id=1, source_target_pairs={{0,8},{8,16},{16,24},{24,32},{32,40},{40,48},{48,56},{56,64},{64,7... | collective-permute-start | bytes 196616 | tf_op jit(solution)/shard_map/ppermute | solution.py:12
  124.5 4.8 %collective-permute-start = (bf16[256,128]{0,1:T(8,128)(2,1)S(1)}, bf16[256,128]{0,1:T(8,128)(2,1)S(1)}, u32[]{:S(2)}, u32[]{:S(2)}) collective-permute-start(bf16[256,128]{0,1:T(8,128)(2,1)S(1)} %pad_maximum_fusion), channel_id=1, source_target_pairs={{0,8},{8,16},{16,24},{24,32},{32,40},{40,48},{48,56},{56,64},{64,7... | collective-permute-start | bytes 196616 | tf_op jit(solution)/shard_map/ppermute | solution.py:12
  328.2 0.8 copy-start.1
  328.2 0.9 copy-start.2
  328.2 0.9 copy-start.3
  328.2 0.9 copy-start.4
  329.6 0.8 copy-start.6
  329.6 0.8 copy-start.11
Sparse Core Ops, SparseCore 0:
  9.5 36.9 all-gather.6
  70.0 80.3 all-gather.10
  153.4 78.7 all-gather.12
  235.1 88.1 all-gather.8
where the time goes:
time: 393 us; the launch traced here: 392 us
  waiting for transfers between devices  158 us (40%)
  blocking collectives  106 us (27%)
  matrix products  52.6 us (13%)
  local copies, waits for them, and re-layouts  45.4 us (12%)
  between operations  15.4 us (4%)
  other arithmetic  8.55 us (2%)
  starting transfers between devices  4.95 us (1%)
    all_gather x1, waiting for transfers between devices, on_device(): lax.all_gather(w_query, 'ctx', axis=0, tiled=True)  88.1 us
    all_gather x1, waiting for transfers between devices, on_device(): lax.all_gather(own_value, 'ctx', axis=0, tiled=True)  66.8 us
    all_gather x1, blocking collectives, on_device(): lax.all_gather(key_weight_matrix, 'ctx', axis=0, tiled=True)  57.6 us
    all_gather x1, blocking collectives, on_device(): lax.all_gather(value_weight_matrix, 'ctx', axis=0, tiled=True)  48.6 us
    gather x1, local copies, waits for them, and re-layouts, on_device(): near_key = prior_key[slash_index]  14.9 us
    gather x1, local copies, waits for them, and re-layouts, on_device(): near_value = prior_value[slash_index]  14.9 us
    dot_general x7, matrix products, one_head(): jnp.einsum('td,tnd->tn', near_q, near_key, preferred_element_type=jnp.flo...  13 us
    dot_general x7, matrix products, one_head(): jnp.einsum('tn,tnd->td', weight_near, near_value, preferred_element_type=...  11.4 us
  transfers between devices with their start and end apart: 6, of which 3 were waited for; matrix products, arithmetic and copies ran while one was open for 11% of the time, Pallas kernels for 0%

commit v1 on v0

v1 whole, which is shorter than its diff:
```python
import functools

import jax
import jax.numpy as jnp
import numpy as np
from jax import lax
from jax.experimental import pallas as pl
from jax.experimental.pallas import tpu as pltpu
from jax.sharding import PartitionSpec as P

BLOCK = 128
SIDE = 8
MASKED = -1e30
LOG2E = 1.4426950408889634
BF16, F32 = jnp.bfloat16, jnp.float32


def rope_tables(tokens, width):
    exponents = np.arange(0, width, 2).astype(np.float32) / np.float32(width)
    inverse = np.power(np.float32(10000000.0), -exponents).astype(np.float32)
    places = np.arange(tokens).astype(np.float32)

    def pair(positions):
        angles = (positions[:, None] * inverse[None, :]).astype(np.float32).astype(np.float64)
        cosine, sine = np.cos(angles), np.sin(angles)
        return [
            np.concatenate([cosine, cosine], axis=1).astype(np.float32),
            np.concatenate([-sine, sine], axis=1).astype(np.float32),
        ]

    moving = np.stack(pair(places) + pair(places + np.float32(tokens)))
    fixed = np.concatenate(pair(np.full((1,), 2 * tokens - 1, np.float32)))
    return moving, fixed


def rotate(rows, cosine, sine):
    return rows * cosine + pltpu.roll(rows, rows.shape[-1] // 2, axis=1) * sine


def kernel(
    hid, wk, wv, wq, bq, bk, bv, published, vertical, vcount, slash, scount, moving, fixed,
    out,
    hbuf, wkb, wvb, wq0, wq1, pool, kt, vv, qraw, ql, qn, qf, kft, vft,
    top1, sum1, acc1, bias_local, bias_near,
    send, recv, lsem,
):
    tokens, part = hid.shape
    width = wk.shape[1]
    group = wq.shape[1] // width
    left_cols = wq0.shape[-1]
    heads = hbuf.shape[0]
    x, c, r = lax.axis_index("head"), lax.axis_index("ctx"), lax.axis_index("row")
    y, z = c // SIDE, c % SIDE
    score_scale = width**-0.5 * LOG2E

    def at(yy, zz):
        return {"ctx": ((yy + SIDE) % SIDE) * SIDE + (zz + SIDE) % SIDE}

    sibling = {"row": 1 - r}
    x_right, x_left = {"head": (x + 1) % heads}, {"head": (x + heads - 1) % heads}
    span_next, span_prior = {"ctx": (c + 1) % SIDE**2}, {"ctx": (c + SIDE**2 - 1) % SIDE**2}

    def per_row(body):
        for rr in range(2):
            pl.when(r == rr)(functools.partial(body, rr))

    ids = {}

    def sem(*name):
        return ids.setdefault(name, len(ids))

    def copy(name, src, dst, device):
        index = sem(*name)
        return pltpu.make_async_remote_copy(
            src_ref=src,
            dst_ref=dst,
            send_sem=send.at[index],
            recv_sem=recv.at[index],
            device_id=device,
            device_id_type=pl.DeviceIdType.MESH,
        )

    class Stream:
        def __init__(self, name, bufs, share):
            self.name, self.bufs, self.share = name, bufs, share

        def slot(self, rr, i):
            return self.bufs[rr].at[y, i] if rr == 0 else self.bufs[rr].at[i, z]

        def unit(self, rr, i, sub):
            cut = pl.ds(sub * (SIDE // 2), SIDE // 2)
            return self.bufs[rr].at[i, cut] if rr == 0 else self.bufs[rr].at[cut, i]

        def row_unit(self, rr):
            return self.bufs[rr].at[y] if rr == 0 else self.bufs[rr].at[:, z]

        def first(self, rr, way, step, arriving):
            pos = z if rr == 0 else y
            i = (pos - way * (step if arriving else step - 1) + SIDE) % SIDE
            ref = self.slot(rr, i)
            device = at(y, z + way) if rr == 0 else at(y + way, z)
            return copy((self.name, "first", way, step), ref, ref, device)

        def second(self, rr, way, step, sub, arriving):
            pos = y if rr == 0 else z
            i = (pos - way * (step if arriving else step - 1) + SIDE) % SIDE
            ref = self.unit(rr, i, sub)
            device = at(y + way, z) if rr == 0 else at(y, z + way)
            return copy((self.name, "second", way, step, sub), ref, ref, device)

        def to_sibling(self, rr, way, step, sub):
            pos = y if rr == 0 else z
            if step == 0:
                ref = self.row_unit(rr)
            else:
                ref = self.unit(rr, (pos - way * step + SIDE) % SIDE, sub)
            return copy((self.name, "sibling", way, step, sub), ref, ref, sibling)

        def shared(self):
            return [(0, 0, 0)] + [(w, s, b) for w, s, b in self.seconds()]

        @staticmethod
        def firsts():
            return [(1, s) for s in (1, 2, 3, 4)] + [(-1, s) for s in (1, 2, 3)]

        @staticmethod
        def seconds():
            some = [(w, s, b) for s in (1, 2, 3) for b in (0, 1) for w in (1, -1)]
            return some + [(1, 4, 0), (-1, 4, 1)]

        def first_begin(self, rr):
            for way in (1, -1):
                self.first(rr, way, 1, False).start()

        def first_step(self, rr, step):
            for way in (1, -1):
                if (way, step) in self.firsts():
                    self.first(rr, way, step, True).wait_recv()
                    if (way, step + 1) in self.firsts():
                        self.first(rr, way, step + 1, False).start()

        def second_begin(self, rr):
            for sub in (0, 1):
                for way in (1, -1):
                    self.second(rr, way, 1, sub, False).start()
            if self.share:
                self.to_sibling(rr, 0, 0, 0).start()

        def second_step(self, rr, step, sub):
            for way in (1, -1):
                if (way, step, sub) in self.seconds():
                    self.second(rr, way, step, sub, True).wait_recv()
                    if (way, step + 1, sub) in self.seconds():
                        self.second(rr, way, step + 1, sub, False).start()
                    if self.share:
                        self.to_sibling(rr, way, step, sub).start()

        def from_sibling(self, rr):
            for way, step, sub in self.shared():
                self.to_sibling(1 - rr, way, step, sub).wait_recv()

        def finish(self, rr):
            for way, step in self.firsts():
                self.first(rr, way, step, False).wait_send()
            for way, step, sub in self.seconds():
                self.second(rr, way, step, sub, False).wait_send()
            if self.share:
                for way, step, sub in self.shared():
                    self.to_sibling(rr, way, step, sub).wait_send()

    kv_stream = Stream("kv", (wkb, wvb), True)
    q_stream = Stream("q", (wq0, wq1), True)
    pool_stream = Stream("pool", (pool, pool), False)

    own_hidden = pltpu.make_async_copy(hid, hbuf.at[x], lsem.at[0])
    own_hidden.start()

    def own_weights(rr):
        columns = pl.ds(0, left_cols) if rr == 0 else pl.ds(left_cols, wq.shape[1] - left_cols)
        return (
            pltpu.make_async_copy((wk, wv)[rr], (wkb, wvb)[rr].at[y, z], lsem.at[1]),
            pltpu.make_async_copy(wq.at[:, columns], (wq0, wq1)[rr].at[y, z], lsem.at[2]),
        )

    per_row(lambda rr: [one.start() for one in own_weights(rr)] and None)

    barrier = pltpu.get_barrier_semaphore()
    partners = (
        at(y, z + 1), at(y, z - 1), at(y + 1, z), at(y - 1, z),
        sibling, x_right, x_left, span_next, span_prior,
    )
    for device in partners:
        pl.semaphore_signal(barrier, inc=1, device_id=device, device_id_type=pl.DeviceIdType.MESH)
    pl.semaphore_wait(barrier, len(partners))

    half = tokens // 2

    def feature(way, sub, far, arriving):
        away = way * ((2 if far else 1) if arriving else (1 if far else 0))
        ref = hbuf.at[(x - away + heads) % heads, pl.ds(sub * half, half)]
        return copy(("x", way, sub, far), ref, ref, x_right if way == 1 else x_left)

    own_hidden.wait()
    for way, sub in ((1, 0), (-1, 1), (1, 1), (-1, 0)):
        feature(way, sub, False, False).start()

    def weights_begin(rr):
        first, second = own_weights(rr)
        first.wait()
        kv_stream.first_begin(rr)
        second.wait()
        q_stream.first_begin(rr)

    per_row(weights_begin)

    rows = lax.broadcasted_iota(jnp.int32, (tokens, tokens), 0)
    columns = lax.broadcasted_iota(jnp.int32, (tokens, tokens), 1)
    bias_local[...] = jnp.where(rows >= columns, 0.0, MASKED)
    back = rows - columns + tokens
    near = jnp.full((tokens, tokens), MASKED, F32)
    for e in range(slash.shape[-1]):
        offset = jnp.where((e < scount[0, 0]) & (c > 0), slash[0, 0, e], 0)
        near = jnp.where(back == offset, 0.0, near)
    bias_near[...] = near

    def weights_first(rr):
        for step in (1, 2, 3, 4):
            kv_stream.first_step(rr, step)
            if step == 4:
                kv_stream.second_begin(rr)
            q_stream.first_step(rr, step)
        q_stream.second_begin(rr)

    per_row(weights_first)
    for way, sub in ((1, 0), (-1, 1)):
        feature(way, sub, False, True).wait_recv()
        feature(way, sub, True, False).start()

    def weights_second(rr):
        for step in (1, 2, 3, 4):
            for sub in (0, 1):
                kv_stream.second_step(rr, step, sub)
        for sub in (0, 1):
            q_stream.second_step(rr, 1, sub)
        kv_stream.from_sibling(rr)

    per_row(weights_second)
    for way, sub in ((1, 1), (-1, 0)):
        feature(way, sub, False, True).wait_recv()
    for way, sub in ((1, 0), (-1, 1)):
        feature(way, sub, True, True).wait_recv()

    def project(h, weights):
        rows_of = weights.at[pl.ds(2 * h, 2)][...]
        block = rows_of.reshape(part, rows_of.shape[-1])
        return jnp.dot(hbuf[h], block, preferred_element_type=F32)

    def project_all(weights):
        total = project(0, weights)
        for h in range(1, heads):
            total = total + project(h, weights)
        return total

    keys = rotate(project_all(wkb) + bk[...], moving[0], moving[1]).astype(BF16)
    kt[0] = keys.T
    vv[0] = (project_all(wvb) + bv[...]).astype(BF16)
    behind = [
        copy(("prior", "k"), kt.at[0], kt.at[1], span_next),
        copy(("prior", "v"), vv.at[0], vv.at[1], span_next),
    ]
    for one in behind:
        one.start()
    first_block = published[0, 0] == 0
    pool[y, z, 0] = jnp.where(first_block, kt[0, :, :BLOCK], kt[0, :, BLOCK:])
    pool[y, z, 1] = jnp.where(first_block, vv[0, :BLOCK], vv[0, BLOCK:])

    def middle(rr):
        pool_stream.first_begin(rr)
        for sub in (0, 1):
            q_stream.second_step(rr, 2, sub)
        for step in (1, 2):
            pool_stream.first_step(rr, step)
        for sub in (0, 1):
            q_stream.second_step(rr, 3, sub)
        for step in (3, 4):
            pool_stream.first_step(rr, step)
        pool_stream.second_begin(rr)
        for sub in (0, 1):
            q_stream.second_step(rr, 4, sub)
        q_stream.from_sibling(rr)

    per_row(middle)

    def pool_step(step, sub):
        per_row(lambda rr: pool_stream.second_step(rr, step, sub))

    qraw[:, :left_cols] = project_all(wq0)
    pool_step(1, 0)
    qraw[:, left_cols:] = project_all(wq1)
    pool_step(1, 1)

    def rotate_head(g):
        columns = pl.ds(pl.multiple_of(g * width, width), width)
        raw = qraw[:, columns] + bq[:, columns]
        swapped = pltpu.roll(raw, width // 2, axis=1)
        ql[g] = (raw * moving[0] + swapped * moving[1]).astype(BF16)
        qn[g] = (raw * moving[2] + swapped * moving[3]).astype(BF16)
        qf[g] = (raw * fixed[0:1] + swapped * fixed[1:2]).astype(BF16)

    pl.loop(0, group)(rotate_head)
    pool_step(2, 0)
    for one in behind:
        one.wait_recv()

    def close_part(g):
        local = jnp.dot(ql[g], kt[0], preferred_element_type=F32) * score_scale + bias_local[...]
        slashed = jnp.dot(qn[g], kt[1], preferred_element_type=F32) * score_scale + bias_near[...]
        highest = jnp.maximum(
            jnp.max(local, axis=1, keepdims=True), jnp.max(slashed, axis=1, keepdims=True)
        )
        local, slashed = jnp.exp2(local - highest), jnp.exp2(slashed - highest)
        total = jnp.sum(local, axis=1, keepdims=True) + jnp.sum(slashed, axis=1, keepdims=True)
        top1[g] = jnp.broadcast_to(highest, (tokens, width))
        sum1[g] = jnp.broadcast_to(total, (tokens, width))
        acc1[g] = jnp.dot(local.astype(BF16), vv[0], preferred_element_type=F32) + jnp.dot(
            slashed.astype(BF16), vv[1], preferred_element_type=F32
        )

    for start, stop, step, sub in ((0, 2, 2, 1), (2, 4, 3, 0), (4, 6, 3, 1), (6, group, 4, 0)):
        pl.loop(start, stop)(close_part)
        pool_step(step, sub)
    pool_step(4, 1)

    slots = vertical.shape[-1]
    for e in range(slots):
        span = vertical[0, 0, e]
        kft[:, e * BLOCK : (e + 1) * BLOCK] = pool[span // SIDE, span % SIDE, 0]
        vft[e * BLOCK : (e + 1) * BLOCK] = pool[span // SIDE, span % SIDE, 1]
    place = lax.broadcasted_iota(jnp.int32, (1, slots * BLOCK), 1)
    bias_far = jnp.where(place < vcount[0, 0] * BLOCK, 0.0, MASKED)

    def far_part(g):
        scores = jnp.dot(qf[g], kft[...], preferred_element_type=F32) * score_scale + bias_far
        before = top1[g][:, :1]
        highest = jnp.maximum(before, jnp.max(scores, axis=1, keepdims=True))
        weights = jnp.exp2(scores - highest)
        fade = jnp.exp2(before - highest)
        total = sum1[g][:, :1] * fade + jnp.sum(weights, axis=1, keepdims=True)
        combined = acc1[g] * fade + jnp.dot(
            weights.astype(BF16), vft[...], preferred_element_type=F32
        )
        columns = pl.ds(pl.multiple_of(g * width, width), width)
        out[:, columns] = (combined / total).astype(BF16)

    pl.loop(0, group)(far_part)

    for way, sub in ((1, 0), (-1, 1), (1, 1), (-1, 0)):
        feature(way, sub, False, False).wait_send()
    for way, sub in ((1, 0), (-1, 1)):
        feature(way, sub, True, False).wait_send()
    for one in behind:
        one.wait_send()
    per_row(lambda rr: [s.finish(rr) for s in (kv_stream, q_stream, pool_stream)] and None)


def on_device(
    hidden_states, w_query, key_weight_matrix, value_weight_matrix, bias_query, bias_key,
    value_bias_vector, published, vertical, vcount, slash_offsets, scount,
):
    tokens, part = hidden_states.shape
    depth, width = key_weight_matrix.shape
    columns = w_query.shape[1]
    group = columns // width
    heads = lax.axis_size("head")
    slots = vertical.shape[-1]
    left = (group // 2) * width
    moving, fixed = rope_tables(tokens, width)
    hbm = pl.BlockSpec(memory_space=pl.ANY)
    vmem = pl.BlockSpec(memory_space=pltpu.VMEM)
    smem = pl.BlockSpec(memory_space=pltpu.SMEM)
    copies = 160
    return pl.pallas_call(
        kernel,
        out_shape=jax.ShapeDtypeStruct((tokens, columns), BF16),
        in_specs=[hbm] * 4 + [vmem] * 3 + [smem] * 5 + [vmem] * 2,
        out_specs=vmem,
        scratch_shapes=[
            pltpu.VMEM((heads, tokens, part), BF16),
            pltpu.VMEM((SIDE, SIDE, depth, width), BF16),
            pltpu.VMEM((SIDE, SIDE, depth, width), BF16),
            pltpu.VMEM((SIDE, SIDE, depth, left), BF16),
            pltpu.VMEM((SIDE, SIDE, depth, columns - left), BF16),
            pltpu.VMEM((SIDE, SIDE, 2, BLOCK, width), BF16),
            pltpu.VMEM((2, width, tokens), BF16),
            pltpu.VMEM((2, tokens, width), BF16),
            pltpu.VMEM((tokens, columns), F32),
            pltpu.VMEM((group, tokens, width), BF16),
            pltpu.VMEM((group, tokens, width), BF16),
            pltpu.VMEM((group, tokens, width), BF16),
            pltpu.VMEM((width, slots * BLOCK), BF16),
            pltpu.VMEM((slots * BLOCK, width), BF16),
            pltpu.VMEM((group, tokens, width), F32),
            pltpu.VMEM((group, tokens, width), F32),
            pltpu.VMEM((group, tokens, width), F32),
            pltpu.VMEM((tokens, tokens), F32),
            pltpu.VMEM((tokens, tokens), F32),
            pltpu.SemaphoreType.DMA((copies,)),
            pltpu.SemaphoreType.DMA((copies,)),
            pltpu.SemaphoreType.DMA((3,)),
        ],
        compiler_params=pltpu.CompilerParams(
            collective_id=0, has_side_effects=True, vmem_limit_bytes=56 * 1024 * 1024
        ),
        cost_estimate=pl.CostEstimate(
            flops=4 * 10**9, bytes_accessed=10**7, transcendentals=3 * 10**6
        ),
    )(
        hidden_states, key_weight_matrix, value_weight_matrix, w_query,
        bias_query.reshape(1, columns), bias_key.reshape(1, width),
        value_bias_vector.reshape(1, width),
        published, vertical, vcount, slash_offsets, scount,
        jnp.asarray(moving), jnp.asarray(fixed),
    )


def solution(mesh):
    spans, kept = P(("row", "ctx"), "head"), P(("row", "ctx"), "head", None)
    weight, bias = P("ctx", "head"), P("head")
    return jax.shard_map(
        on_device,
        mesh=mesh,
        in_specs=(spans, weight, weight, weight, bias, bias, bias, spans, kept, spans, kept, spans),
        out_specs=spans,
        check_vma=False,
    )
```

time: 393 us -> 101 us (0.26)
  waiting for transfers between devices: 158 us -> 0 us
  blocking collectives: 106 us -> 0 us
  Pallas kernels: 0 us -> 96.1 us
  matrix products: 52.6 us -> 0 us
  local copies, waits for them, and re-layouts: 45.4 us -> 2.41 us
  between operations: 15.4 us -> 1.98 us
  other arithmetic: 8.55 us -> 0 us
  starting transfers between devices: 4.95 us -> 0 us
    all_gather x4 -> x0, waiting for transfers between devices: 155 us -> none  [the longest x1 88.1 us: on_device(): lax.all_gather(w_query, 'ctx', axis=0, tiled=True)]
    all_gather x2 -> x0, blocking collectives: 106 us -> none  [the longest x1 57.6 us: on_device(): lax.all_gather(key_weight_matrix, 'ctx', axis=0, tiled=True)]
    pallas_call x0 -> x1, Pallas kernels: none -> 96.1 us  [on_device(): pl.pallas_call(kernel, out_shape=jax.ShapeDtypeStruct((tokens, columns),...]
    dot_general x45 -> x0, matrix products: 52.6 us -> none  [the longest x7 13 us: one_head(): jnp.einsum('td,tnd->tn', near_q, near_key, preferred_element_type=jnp.flo...]
    gather x4 -> x0, local copies, waits for them, and re-layouts: 34.2 us -> none  [the longest x1 14.9 us: on_device(): near_key = prior_key[slash_index]]
    ppermute x2 -> x0, starting transfers between devices: 4.82 us -> none  [from_behind(): return lax.ppermute(block, axis, route)]
    all_gather x1 -> x0, local copies, waits for them, and re-layouts: 4.09 us -> none  [on_device(): lax.all_gather(own_key, 'ctx', axis=0, tiled=True)]
  transfers between devices with their start and end apart: 6 -> 0, of which waited for: 3 -> 0; matrix products, arithmetic and copies ran while one was open for 11% -> 0% of each run, Pallas kernels for 0% -> 0%
where the time goes in v1:
time: 101 us; the launch traced here: 100 us
  Pallas kernels  96.1 us (95%)
  local copies, waits for them, and re-layouts  2.41 us (2%)
  between operations  1.98 us (2%)
    pallas_call x1, Pallas kernels, on_device(): pl.pallas_call(kernel, out_shape=jax.ShapeDtypeStruct((tokens, columns),...  96.1 us

profile of v1, /device:TPU:6, one launch (start us, length us, event | category | flops | bytes accessed | tf_op | source)
XLA Modules:
  0.0 100.5 jit_solution(17824394555368408357)
XLA Ops:
  0.7 0.0 copy-start
  2.0 0.0 copy-done
  2.0 0.6 reshape.9.bq
  2.6 96.1 %shard_map.136 = bf16[256,896]{1,0:T(8,128)(2,1)} custom-call(bf16[256,896]{1,0:T(8,128)(2,1)} %hid.1, bf16[56,128]{1,0:T(8,128)(2,1)} %wk.1, bf16[56,128]{1,0:T(8,128)(2,1)} %wv.1, bf16[56,896]{1,0:T(8,128)(2,1)} %wq.1, f32[1,896]{1,0:T(1,128)} %reshape.9.bq, f32[1,128]{1,0:T(1,128)} %bitcast.2, f32[1,128]{1,0:T(1,128)} %bitcast.3, ...), custom_call_target="tpu_custom_call" | custom-call | flops 4000000000 | bytes 10000000 | tf_op jit(solution)/shard_map/pallas_call | solution.py:382
  98.6 1.8 %copy.19 = bf16[256,896]{1,0:T(8,128)(2,1)} copy(bf16[256,896]{1,0:T(8,128)(2,1)} %shard_map.136) | data formatting | bytes 917504
Async XLA Ops:
  0.7 1.3 %copy-start = (f32[896]{0:T(1024)S(1)}, f32[896]{0:T(1024)}, u32[]{:S(2)}) copy-start(f32[896]{0:T(1024)} %param.18) | copy-start | bytes 10756

commit v2 on v1

v2 whole, which is shorter than its diff:
```python
import functools

import jax
import jax.numpy as jnp
import numpy as np
from jax import lax
from jax.experimental import pallas as pl
from jax.experimental.pallas import tpu as pltpu
from jax.sharding import PartitionSpec as P

BLOCK = 128
SIDE = 8
MASKED = -1e30
FIRST_ORDER = (4, 3, -3, 2, -2, 1, -1)
LOG2E = 1.4426950408889634
BF16, F32 = jnp.bfloat16, jnp.float32


def rope_tables(tokens, width):
    exponents = np.arange(0, width, 2).astype(np.float32) / np.float32(width)
    inverse = np.power(np.float32(10000000.0), -exponents).astype(np.float32)
    places = np.arange(tokens).astype(np.float32)

    def pair(positions):
        angles = (positions[:, None] * inverse[None, :]).astype(np.float32).astype(np.float64)
        cosine, sine = np.cos(angles), np.sin(angles)
        return [
            np.concatenate([cosine, cosine], axis=1).astype(np.float32),
            np.concatenate([-sine, sine], axis=1).astype(np.float32),
        ]

    moving = np.stack(pair(places) + pair(places + np.float32(tokens)))
    fixed = np.concatenate(pair(np.full((1,), 2 * tokens - 1, np.float32)))
    return moving, fixed


def rotate(rows, cosine, sine):
    return rows * cosine + pltpu.roll(rows, rows.shape[-1] // 2, axis=1) * sine


def kernel(
    hid, wk, wv, wq, bq, bk, bv, published, vertical, vcount, slash, scount, listed, moving, fixed,
    out,
    hbuf, wkb, wvb, wq0, wq1, pool, chosen, got, lists, kt, vv, qraw, ql, qn, qf, kft, vft,
    top1, sum1, acc1, bias_local, bias_near,
    send, recv, lsem,
):
    tokens, part = hid.shape
    width = wk.shape[1]
    group = wq.shape[1] // width
    left_cols = wq0.shape[-1]
    heads = hbuf.shape[0]
    slots = vertical.shape[-1]
    x, c, r = lax.axis_index("head"), lax.axis_index("ctx"), lax.axis_index("row")
    y, z = c // SIDE, c % SIDE
    score_scale = width**-0.5 * LOG2E

    def at(yy, zz):
        return {"ctx": ((yy + SIDE) % SIDE) * SIDE + (zz + SIDE) % SIDE}

    sibling = {"row": 1 - r}
    x_right, x_left = {"head": (x + 1) % heads}, {"head": (x + heads - 1) % heads}
    span_next, span_prior = {"ctx": (c + 1) % SIDE**2}, {"ctx": (c + SIDE**2 - 1) % SIDE**2}

    pos1, pos2 = jnp.where(r == 0, z, y), jnp.where(r == 0, y, z)

    def along1(d):
        there = (pos1 + d + SIDE) % SIDE
        return {"ctx": jnp.where(r == 0, y * SIDE + there, there * SIDE + z)}

    def along2(d):
        there = (pos2 + d + SIDE) % SIDE
        return {"ctx": jnp.where(r == 0, there * SIDE + z, y * SIDE + there)}

    def per_row(body):
        for rr in range(2):
            pl.when(r == rr)(functools.partial(body, rr))

    ids = {}

    def copy(name, src, dst, device):
        index = ids.setdefault(name, len(ids))
        return pltpu.make_async_remote_copy(
            src_ref=src,
            dst_ref=dst,
            send_sem=send.at[index],
            recv_sem=recv.at[index],
            device_id=device,
            device_id_type=pl.DeviceIdType.MESH,
        )

    class Weights:
        def __init__(self, name, bufs):
            self.name, self.bufs = name, bufs

        def slot(self, rr, i):
            return self.bufs[rr].at[y, i] if rr == 0 else self.bufs[rr].at[i, z]

        def unit(self, rr, away, sub=None):
            i = (pos2 + away + SIDE) % SIDE
            if sub is None:
                return self.bufs[rr].at[i] if rr == 0 else self.bufs[rr].at[:, i]
            cut = pl.ds(sub * (SIDE // 2), SIDE // 2)
            return self.bufs[rr].at[i, cut] if rr == 0 else self.bufs[rr].at[cut, i]

        def first(self, rr, d, arriving):
            ref = self.slot(rr, (pos1 - d + SIDE) % SIDE if arriving else pos1)
            return copy((self.name, "first", d), ref, ref, along1(d))

        def first_begin(self, rr):
            for d in FIRST_ORDER:
                self.first(rr, d, False).start()

        def first_end(self, rr):
            for d in reversed(FIRST_ORDER):
                self.first(rr, d, True).wait_recv()

        def second(self, rr, move, arriving):
            d, away, sub = move
            ref = self.unit(rr, away - d if arriving else away, sub)
            return copy((self.name, "second", move), ref, ref, along2(d))

        def to_sibling(self, rr, away, sub=None):
            ref = self.unit(rr, away, sub)
            return copy((self.name, "sibling", away, sub), ref, ref, sibling)

        def pass_on(self, rr, move):
            d, away, sub = move
            self.to_sibling(rr, away - d, sub).start()

        def from_sibling(self, rr):
            self.to_sibling(1 - rr, 0).wait_recv()
            for d, away, sub in self.moves:
                self.to_sibling(1 - rr, away - d, sub).wait_recv()

        def finish(self, rr):
            for d in FIRST_ORDER:
                self.first(rr, d, False).wait_send()
            self.to_sibling(rr, 0).wait_send()
            for move in self.moves:
                self.second(rr, move, False).wait_send()
                self.to_sibling(rr, move[1] - move[0], move[2]).wait_send()

    kv, query = Weights("kv", (wkb, wvb)), Weights("q", (wq0, wq1))
    kv.one = [(1, 0, None), (-1, 0, None), (2, 0, None), (-2, 0, None)]
    kv.two = [(1, -2, None), (-1, 2, None), (2, -2, 0), (-2, 2, 1)]
    kv.moves = kv.one + kv.two

    def query_move(way, step, sub):
        return (way, -way * (step - 1), sub)

    query.steps = [(w, s, b) for s in (1, 2, 3) for b in (0, 1) for w in (1, -1)]
    query.steps += [(1, SIDE // 2, 0), (-1, SIDE // 2, 1)]
    query.moves = [query_move(*step) for step in query.steps]

    def query_begin(rr):
        for step in query.steps[:4]:
            query.second(rr, query_move(*step), False).start()
        query.to_sibling(rr, 0).start()

    def query_step(rr, step, sub):
        for way in (1, -1):
            if (way, step, sub) in query.steps:
                query.second(rr, query_move(way, step, sub), True).wait_recv()
                if (way, step + 1, sub) in query.steps:
                    query.second(rr, query_move(way, step + 1, sub), False).start()
                query.pass_on(rr, query_move(way, step, sub))

    own_hidden = pltpu.make_async_copy(hid, hbuf.at[x], lsem.at[0])
    own_hidden.start()

    def own_weights(rr):
        columns = pl.ds(0, left_cols) if rr == 0 else pl.ds(left_cols, wq.shape[1] - left_cols)
        return (
            pltpu.make_async_copy((wk, wv)[rr], (wkb, wvb)[rr].at[y, z], lsem.at[1]),
            pltpu.make_async_copy(wq.at[:, columns], (wq0, wq1)[rr].at[y, z], lsem.at[2]),
        )

    per_row(lambda rr: [one.start() for one in own_weights(rr)] and None)

    barrier = pltpu.get_barrier_semaphore()
    partners = [along1(d) for d in FIRST_ORDER] + [along2(d) for d in (1, -1, 2, -2, 4)]
    partners += [sibling, x_right, x_left, span_next, span_prior]
    for device in partners:
        pl.semaphore_signal(barrier, inc=1, device_id=device, device_id_type=pl.DeviceIdType.MESH)
    pl.semaphore_wait(barrier, len(partners))

    def weights_begin(rr):
        first, second = own_weights(rr)
        first.wait()
        kv.first_begin(rr)
        second.wait()
        query.first_begin(rr)

    per_row(weights_begin)

    half = tokens // 2

    def feature(way, sub, far, arriving):
        away = way * ((2 if far else 1) if arriving else (1 if far else 0))
        ref = hbuf.at[(x - away + heads) % heads, pl.ds(sub * half, half)]
        return copy(("x", way, sub, far), ref, ref, x_right if way == 1 else x_left)

    own_hidden.wait()
    for way, sub in ((1, 0), (-1, 1), (1, 1), (-1, 0)):
        feature(way, sub, False, False).start()

    list_sends = [copy(("list", d), listed, lists.at[i], along2(d)) for i, d in ((0, -1), (1, 1))]
    for one in list_sends:
        one.start()

    rows = lax.broadcasted_iota(jnp.int32, (tokens, tokens), 0)
    columns = lax.broadcasted_iota(jnp.int32, (tokens, tokens), 1)
    bias_local[...] = jnp.where(rows >= columns, 0.0, MASKED)
    back = rows - columns + tokens
    near = jnp.full((tokens, tokens), MASKED, F32)
    for e in range(slash.shape[-1]):
        offset = jnp.where((e < scount[0, 0]) & (c > 0), slash[0, 0, e], 0)
        near = jnp.where(back == offset, 0.0, near)
    bias_near[...] = near

    def kv_first(rr):
        kv.first_end(rr)
        for move in kv.one:
            kv.second(rr, move, False).start()
        kv.to_sibling(rr, 0).start()

    per_row(kv_first)
    for way, sub in ((1, 0), (-1, 1)):
        feature(way, sub, False, True).wait_recv()
        feature(way, sub, True, False).start()

    def spread(rr):
        query.first_end(rr)
        query_begin(rr)
        for move in kv.one:
            kv.second(rr, move, True).wait_recv()
        for move in kv.two:
            kv.second(rr, move, False).start()
        for move in kv.one:
            kv.pass_on(rr, move)
        for sub in (0, 1):
            query_step(rr, 1, sub)
        for move in kv.two:
            kv.second(rr, move, True).wait_recv()
            kv.pass_on(rr, move)
        kv.from_sibling(rr)

    per_row(spread)
    for way, sub in ((1, 1), (-1, 0)):
        feature(way, sub, False, True).wait_recv()
    for way, sub in ((1, 0), (-1, 1)):
        feature(way, sub, True, True).wait_recv()

    def project(h, weights):
        rows_of = weights.at[pl.ds(2 * h, 2)][...]
        block = rows_of.reshape(part, rows_of.shape[-1])
        return jnp.dot(hbuf[h], block, preferred_element_type=F32)

    def project_all(weights):
        total = project(0, weights)
        for h in range(1, heads):
            total = total + project(h, weights)
        return total

    def query_steps(*steps):
        per_row(lambda rr: [query_step(rr, *one) for one in steps] and None)

    keys = rotate(project_all(wkb) + bk[...], moving[0], moving[1]).astype(BF16)
    kt[0] = keys.T
    query_steps((2, 0))
    vv[0] = (project_all(wvb) + bv[...]).astype(BF16)

    here = pool.at[pos1, pos2 // 2]
    first_block = published[0, 0] == 0
    here[0] = jnp.where(first_block, kt[0, :, :BLOCK], kt[0, :, BLOCK:])
    here[1] = jnp.where(first_block, vv[0, :BLOCK], vv[0, BLOCK:])

    def alike(d, arriving):
        place = (pos2 - d + SIDE) % SIDE if arriving else pos2
        ref = pool.at[pos1, place // 2]
        return copy(("alike", d), ref, ref, along2(d))

    def round_first(way, step, sub, arriving):
        i = (pos1 - way * (step if arriving else step - 1) + SIDE) % SIDE
        ref = pool.at[i, pl.ds(2 * sub, 2)]
        return copy(("round", way, step, sub), ref, ref, along1(way))

    def round_step(step, sub):
        for way in (1, -1):
            if (way, step, sub) in query.steps:
                round_first(way, step, sub, True).wait_recv()
                if (way, step + 1, sub) in query.steps:
                    round_first(way, step + 1, sub, False).start()

    for d in (4, 2, -2):
        alike(d, False).start()
    behind = [
        copy(("prior", "k"), kt.at[0], kt.at[1], span_next),
        copy(("prior", "v"), vv.at[0], vv.at[1], span_next),
    ]
    for one in behind:
        one.start()
    query_steps((2, 1), (3, 0), (3, 1))
    for d in (2, -2, 4):
        alike(d, True).wait_recv()
    for step in query.steps[:4]:
        round_first(*step, False).start()
    query_steps((4, 0), (4, 1))
    round_step(1, 0)
    per_row(query.from_sibling)

    qraw[:, :left_cols] = project_all(wq0)
    round_step(1, 1)
    qraw[:, left_cols:] = project_all(wq1)
    round_step(2, 0)

    def rotate_head(g):
        columns = pl.ds(pl.multiple_of(g * width, width), width)
        raw = qraw[:, columns] + bq[columns][None, :]
        swapped = pltpu.roll(raw, width // 2, axis=1)
        ql[g] = (raw * moving[0] + swapped * moving[1]).astype(BF16)
        qn[g] = (raw * moving[2] + swapped * moving[3]).astype(BF16)
        qf[g] = (raw * fixed[0:1] + swapped * fixed[1:2]).astype(BF16)

    pl.loop(0, 4)(rotate_head)
    round_step(2, 1)
    pl.loop(4, group)(rotate_head)
    round_step(3, 0)
    for one in behind:
        one.wait_recv()

    def close_part(g):
        local = jnp.dot(ql[g], kt[0], preferred_element_type=F32) * score_scale + bias_local[...]
        slashed = jnp.dot(qn[g], kt[1], preferred_element_type=F32) * score_scale + bias_near[...]
        highest = jnp.maximum(
            jnp.max(local, axis=1, keepdims=True), jnp.max(slashed, axis=1, keepdims=True)
        )
        local, slashed = jnp.exp2(local - highest), jnp.exp2(slashed - highest)
        total = jnp.sum(local, axis=1, keepdims=True) + jnp.sum(slashed, axis=1, keepdims=True)
        top1[g] = jnp.broadcast_to(highest, (tokens, width))
        sum1[g] = jnp.broadcast_to(total, (tokens, width))
        acc1[g] = jnp.dot(local.astype(BF16), vv[0], preferred_element_type=F32) + jnp.dot(
            slashed.astype(BF16), vv[1], preferred_element_type=F32
        )

    pl.loop(0, 1)(close_part)
    round_step(3, 1)
    pl.loop(1, 2)(close_part)
    round_step(4, 0)
    round_step(4, 1)

    def place_of(span):
        across, down = span % SIDE, span // SIDE
        return jnp.where(r == 0, across, down), jnp.where(r == 0, down, across)

    for one in list_sends:
        one.wait_recv()
    each = slots // 2
    for side in range(2):
        for e in range(each):
            one, two = place_of(lists[side, 0, side * each + e])
            chosen[side, e] = pool[one, two // 2]
    trades = [copy(("trade", d), chosen.at[i], got.at[i], along2(d)) for i, d in ((0, 1), (1, -1))]
    for one in trades:
        one.start()
    pl.loop(2, group)(close_part)
    for one in trades:
        one.wait_recv()

    for e in range(slots):
        one, two = place_of(vertical[0, 0, e])
        same = two % 2 == pos2 % 2
        block = jnp.where(same, pool[one, two // 2], got[e // each, e % each])
        kft[:, e * BLOCK : (e + 1) * BLOCK] = block[0]
        vft[e * BLOCK : (e + 1) * BLOCK] = block[1]
    place = lax.broadcasted_iota(jnp.int32, (1, slots * BLOCK), 1)
    bias_far = jnp.where(place < vcount[0, 0] * BLOCK, 0.0, MASKED)

    def far_part(g):
        scores = jnp.dot(qf[g], kft[...], preferred_element_type=F32) * score_scale + bias_far
        before = top1[g][:, :1]
        highest = jnp.maximum(before, jnp.max(scores, axis=1, keepdims=True))
        weights = jnp.exp2(scores - highest)
        fade = jnp.exp2(before - highest)
        total = sum1[g][:, :1] * fade + jnp.sum(weights, axis=1, keepdims=True)
        combined = acc1[g] * fade + jnp.dot(
            weights.astype(BF16), vft[...], preferred_element_type=F32
        )
        columns = pl.ds(pl.multiple_of(g * width, width), width)
        out[:, columns] = (combined / total).astype(BF16)

    pl.loop(0, group)(far_part)

    for way, sub in ((1, 0), (-1, 1), (1, 1), (-1, 0)):
        feature(way, sub, False, False).wait_send()
    for way, sub in ((1, 0), (-1, 1)):
        feature(way, sub, True, False).wait_send()
    for one in behind + trades + list_sends:
        one.wait_send()
    for d in (4, 2, -2):
        alike(d, False).wait_send()
    for step in query.steps:
        round_first(*step, False).wait_send()
    per_row(lambda rr: [one.finish(rr) for one in (kv, query)] and None)


def on_device(
    hidden_states, w_query, key_weight_matrix, value_weight_matrix, bias_query, bias_key,
    value_bias_vector, published, vertical, vcount, slash_offsets, scount,
):
    tokens, part = hidden_states.shape
    depth, width = key_weight_matrix.shape
    columns = w_query.shape[1]
    group = columns // width
    heads = lax.axis_size("head")
    slots = vertical.shape[-1]
    left = (group // 2) * width
    moving, fixed = rope_tables(tokens, width)
    hbm = pl.BlockSpec(memory_space=pl.ANY)
    vmem = pl.BlockSpec(memory_space=pltpu.VMEM)
    smem = pl.BlockSpec(memory_space=pltpu.SMEM)
    copies = 160
    return pl.pallas_call(
        kernel,
        out_shape=jax.ShapeDtypeStruct((tokens, columns), BF16),
        in_specs=[hbm] * 4 + [vmem] * 3 + [smem] * 5 + [hbm] + [vmem] * 2,
        out_specs=vmem,
        scratch_shapes=[
            pltpu.VMEM((heads, tokens, part), BF16),
            pltpu.VMEM((SIDE, SIDE, depth, width), BF16),
            pltpu.VMEM((SIDE, SIDE, depth, width), BF16),
            pltpu.VMEM((SIDE, SIDE, depth, left), BF16),
            pltpu.VMEM((SIDE, SIDE, depth, columns - left), BF16),
            pltpu.VMEM((SIDE, SIDE // 2, 2, BLOCK, width), BF16),
            pltpu.VMEM((2, slots // 2, 2, BLOCK, width), BF16),
            pltpu.VMEM((2, slots // 2, 2, BLOCK, width), BF16),
            pltpu.SMEM((2, 1, slots), jnp.int32),
            pltpu.VMEM((2, width, tokens), BF16),
            pltpu.VMEM((2, tokens, width), BF16),
            pltpu.VMEM((tokens, columns), F32),
            pltpu.VMEM((group, tokens, width), BF16),
            pltpu.VMEM((group, tokens, width), BF16),
            pltpu.VMEM((group, tokens, width), BF16),
            pltpu.VMEM((width, slots * BLOCK), BF16),
            pltpu.VMEM((slots * BLOCK, width), BF16),
            pltpu.VMEM((group, tokens, width), F32),
            pltpu.VMEM((group, tokens, width), F32),
            pltpu.VMEM((group, tokens, width), F32),
            pltpu.VMEM((tokens, tokens), F32),
            pltpu.VMEM((tokens, tokens), F32),
            pltpu.SemaphoreType.DMA((copies,)),
            pltpu.SemaphoreType.DMA((copies,)),
            pltpu.SemaphoreType.DMA((3,)),
        ],
        compiler_params=pltpu.CompilerParams(
            collective_id=0, has_side_effects=True, vmem_limit_bytes=56 * 1024 * 1024
        ),
        cost_estimate=pl.CostEstimate(
            flops=4 * 10**9, bytes_accessed=10**7, transcendentals=3 * 10**6
        ),
    )(
        hidden_states, key_weight_matrix, value_weight_matrix, w_query,
        bias_query, bias_key.reshape(1, width),
        value_bias_vector.reshape(1, width),
        published, vertical, vcount, slash_offsets, scount,
        vertical[0], jnp.asarray(moving), jnp.asarray(fixed),
    )


def solution(mesh):
    spans, kept = P(("row", "ctx"), "head"), P(("row", "ctx"), "head", None)
    weight, bias = P("ctx", "head"), P("head")
    return jax.shard_map(
        on_device,
        mesh=mesh,
        in_specs=(spans, weight, weight, weight, bias, bias, bias, spans, kept, spans, kept, spans),
        out_specs=spans,
        check_vma=False,
    )
```

time: 101 us -> 91.6 us (0.907)
  Pallas kernels: 96.1 us -> 87.1 us
    pallas_call x1, Pallas kernels: 96.1 us -> 87.1 us  [on_device(): pl.pallas_call(kernel, out_shape=jax.ShapeDtypeStruct((tokens, columns),...]
where the time goes in v2:
time: 91.6 us; the launch traced here: 90.8 us
  Pallas kernels  87.1 us (95%)
  between operations  1.95 us (2%)
  local copies, waits for them, and re-layouts  1.82 us (2%)
    pallas_call x1, Pallas kernels, on_device(): pl.pallas_call(kernel, out_shape=jax.ShapeDtypeStruct((tokens, columns),...  87.1 us

profile of v2, /device:TPU:6, one launch (start us, length us, event | category | flops | bytes accessed | tf_op | source)
XLA Modules:
  0.0 90.8 jit_solution(15914733675825981068)
XLA Ops:
  1.9 87.1 %shard_map.136 = bf16[256,896]{1,0:T(8,128)(2,1)} custom-call(bf16[256,896]{1,0:T(8,128)(2,1)} %hid.1, bf16[56,128]{1,0:T(8,128)(2,1)} %wk.1, bf16[56,128]{1,0:T(8,128)(2,1)} %wv.1, bf16[56,896]{1,0:T(8,128)(2,1)} %wq.1, f32[896]{0:T(1024)} %bq.1, f32[1,128]{1,0:T(1,128)} %bitcast.3, f32[1,128]{1,0:T(1,128)} %bitcast.4, s32[1,1]{1,0:T(1,128)S(6)} %copy.16.published, ...), custom_call_target="tpu_custom_call" | custom-call | flops 4000000000 | bytes 10000000 | tf_op jit(solution)/shard_map/pallas_call | solution.py:424
  89.0 1.8 %copy.19 = bf16[256,896]{1,0:T(8,128)(2,1)} copy(bf16[256,896]{1,0:T(8,128)(2,1)} %shard_map.136) | data formatting | bytes 917504

commit v3 on v2

--- a/solution.py
+++ b/solution.py
@@ -39,11 +39,12 @@
 
 
 def kernel(
-    hid, wk, wv, wq, bq, bk, bv, published, vertical, vcount, slash, scount, listed, moving, fixed,
-    out,
-    hbuf, wkb, wvb, wq0, wq1, pool, chosen, got, lists, kt, vv, qraw, ql, qn, qf, kft, vft,
+    hid, wk, wv, wq, moving_hbm, published_hbm, vertical_hbm, vcount_hbm, slash_hbm, scount_hbm,
+    bq, bk, bv, fixed,
+    out_hbm,
+    out, moving, published, vertical, vcount, slash, scount, hbuf, wkb, wvb, wq0, wq1, pool, chosen, got, lists, kt, vv, qraw, ql, qn, qf, kft, vft,
     top1, sum1, acc1, bias_local, bias_near,
-    send, recv, lsem,
+    send, recv, lsem, osem,
 ):
     tokens, part = hid.shape
     width = wk.shape[1]
@@ -103,17 +104,18 @@
             cut = pl.ds(sub * (SIDE // 2), SIDE // 2)
             return self.bufs[rr].at[i, cut] if rr == 0 else self.bufs[rr].at[cut, i]
 
-        def first(self, rr, d, arriving):
-            ref = self.slot(rr, (pos1 - d + SIDE) % SIDE if arriving else pos1)
-            return copy((self.name, "first", d), ref, ref, along1(d))
-
-        def first_begin(self, rr):
-            for d in FIRST_ORDER:
-                self.first(rr, d, False).start()
-
-        def first_end(self, rr):
-            for d in reversed(FIRST_ORDER):
-                self.first(rr, d, True).wait_recv()
+        def first(self, rr, move, arriving):
+            d, away = move
+            ref = self.slot(rr, (pos1 + (away - d if arriving else away) + SIDE) % SIDE)
+            return copy((self.name, "first", move), ref, ref, along1(d))
+
+        def first_begin(self, rr, moves):
+            for move in moves:
+                self.first(rr, move, False).start()
+
+        def first_end(self, rr, moves):
+            for move in reversed(moves):
+                self.first(rr, move, True).wait_recv()
 
         def second(self, rr, move, arriving):
             d, away, sub = move
@@ -134,14 +136,16 @@
                 self.to_sibling(1 - rr, away - d, sub).wait_recv()
 
         def finish(self, rr):
-            for d in FIRST_ORDER:
-                self.first(rr, d, False).wait_send()
+            for move in self.near + self.far:
+                self.first(rr, move, False).wait_send()
             self.to_sibling(rr, 0).wait_send()
             for move in self.moves:
                 self.second(rr, move, False).wait_send()
                 self.to_sibling(rr, move[1] - move[0], move[2]).wait_send()
 
     kv, query = Weights("kv", (wkb, wvb)), Weights("q", (wq0, wq1))
+    kv.near, kv.far = [(d, 0) for d in FIRST_ORDER], []
+    query.near, query.far = [(2, 0), (-2, 0), (1, 0), (-1, 0)], [(2, -2), (1, -2), (-1, 2)]
     kv.one = [(1, 0, None), (-1, 0, None), (2, 0, None), (-2, 0, None)]
     kv.two = [(1, -2, None), (-1, 2, None), (2, -2, 0), (-2, 2, 1)]
     kv.moves = kv.one + kv.two
@@ -153,10 +157,9 @@
     query.steps += [(1, SIDE // 2, 0), (-1, SIDE // 2, 1)]
     query.moves = [query_move(*step) for step in query.steps]
 
-    def query_begin(rr):
-        for step in query.steps[:4]:
-            query.second(rr, query_move(*step), False).start()
-        query.to_sibling(rr, 0).start()
+    def query_begin(rr, sub):
+        for way in (1, -1):
+            query.second(rr, query_move(way, 1, sub), False).start()
 
     def query_step(rr, step, sub):
         for way in (1, -1):
@@ -168,6 +171,22 @@
 
     own_hidden = pltpu.make_async_copy(hid, hbuf.at[x], lsem.at[0])
     own_hidden.start()
+    tables = pltpu.make_async_copy(moving_hbm, moving, lsem.at[3])
+    tables.start()
+    small = [
+        pltpu.make_async_copy(src, dst, lsem.at[4 + i])
+        for i, (src, dst) in enumerate(
+            (
+                (published_hbm, published),
+                (vertical_hbm, vertical),
+                (vcount_hbm, vcount),
+                (slash_hbm, slash),
+                (scount_hbm, scount),
+            )
+        )
+    ]
+    for one in small:
+        one.start()
 
     def own_weights(rr):
         columns = pl.ds(0, left_cols) if rr == 0 else pl.ds(left_cols, wq.shape[1] - left_cols)
@@ -188,9 +207,9 @@
     def weights_begin(rr):
         first, second = own_weights(rr)
         first.wait()
-        kv.first_begin(rr)
+        kv.first_begin(rr, kv.near)
         second.wait()
-        query.first_begin(rr)
+        query.first_begin(rr, query.near)
 
     per_row(weights_begin)
 
@@ -205,9 +224,13 @@
     for way, sub in ((1, 0), (-1, 1), (1, 1), (-1, 0)):
         feature(way, sub, False, False).start()
 
-    list_sends = [copy(("list", d), listed, lists.at[i], along2(d)) for i, d in ((0, -1), (1, 1))]
+    list_sends = [copy(("list", d), vertical_hbm.at[0], lists.at[i], along2(d)) for i, d in ((0, -1), (1, 1))]
     for one in list_sends:
         one.start()
+
+    for one in small:
+        one.wait()
+    tables.wait()
 
     rows = lax.broadcasted_iota(jnp.int32, (tokens, tokens), 0)
     columns = lax.broadcasted_iota(jnp.int32, (tokens, tokens), 1)
@@ -220,10 +243,12 @@
     bias_near[...] = near
 
     def kv_first(rr):
-        kv.first_end(rr)
+        kv.first_end(rr, kv.near)
         for move in kv.one:
             kv.second(rr, move, False).start()
         kv.to_sibling(rr, 0).start()
+        query.first_end(rr, query.near)
+        query.first_begin(rr, query.far)
 
     per_row(kv_first)
     for way, sub in ((1, 0), (-1, 1)):
@@ -231,19 +256,21 @@
         feature(way, sub, True, False).start()
 
     def spread(rr):
-        query.first_end(rr)
-        query_begin(rr)
+        query.first_end(rr, query.far)
+        query_begin(rr, 0)
         for move in kv.one:
             kv.second(rr, move, True).wait_recv()
         for move in kv.two:
             kv.second(rr, move, False).start()
+        query_begin(rr, 1)
         for move in kv.one:
             kv.pass_on(rr, move)
-        for sub in (0, 1):
-            query_step(rr, 1, sub)
+        query.to_sibling(rr, 0).start()
+        query_step(rr, 1, 0)
         for move in kv.two:
             kv.second(rr, move, True).wait_recv()
             kv.pass_on(rr, move)
+        query_step(rr, 1, 1)
         kv.from_sibling(rr)
 
     per_row(spread)
@@ -252,24 +279,24 @@
     for way, sub in ((1, 0), (-1, 1)):
         feature(way, sub, True, True).wait_recv()
 
-    def project(h, weights):
-        rows_of = weights.at[pl.ds(2 * h, 2)][...]
-        block = rows_of.reshape(part, rows_of.shape[-1])
+    def project(h, *weights):
+        parts = [one.at[pl.ds(2 * h, 2)][...] for one in weights]
+        block = jnp.concatenate([one.reshape(part, one.shape[-1]) for one in parts], axis=1)
         return jnp.dot(hbuf[h], block, preferred_element_type=F32)
 
-    def project_all(weights):
-        total = project(0, weights)
+    def project_all(*weights):
+        total = project(0, *weights)
         for h in range(1, heads):
-            total = total + project(h, weights)
+            total = total + project(h, *weights)
         return total
 
     def query_steps(*steps):
         per_row(lambda rr: [query_step(rr, *one) for one in steps] and None)
 
-    keys = rotate(project_all(wkb) + bk[...], moving[0], moving[1]).astype(BF16)
+    both = project_all(wkb, wvb)
+    keys = rotate(both[:, :width] + bk[...][None, :], moving[0], moving[1]).astype(BF16)
     kt[0] = keys.T
-    query_steps((2, 0))
-    vv[0] = (project_all(wvb) + bv[...]).astype(BF16)
+    vv[0] = (both[:, width:] + bv[...][None, :]).astype(BF16)
 
     here = pool.at[pos1, pos2 // 2]
     first_block = published[0, 0] == 0
@@ -281,39 +308,61 @@
         ref = pool.at[pos1, place // 2]
         return copy(("alike", d), ref, ref, along2(d))
 
-    def round_first(way, step, sub, arriving):
+    offsets = (0, 2, -2, 4)
+
+    def around(way, step, o, arriving):
         i = (pos1 - way * (step if arriving else step - 1) + SIDE) % SIDE
-        ref = pool.at[i, pl.ds(2 * sub, 2)]
-        return copy(("round", way, step, sub), ref, ref, along1(way))
-
-    def round_step(step, sub):
+        ref = pool.at[i, (pos2 + o + SIDE) % SIDE // 2]
+        return copy(("round", way, step, o), ref, ref, along1(way))
+
+    def ways(step, o):
+        return (1, -1) if step < SIDE // 2 else (1,) if o in (0, 2) else (-1,)
+
+    def round_begin(o):
         for way in (1, -1):
-            if (way, step, sub) in query.steps:
-                round_first(way, step, sub, True).wait_recv()
-                if (way, step + 1, sub) in query.steps:
-                    round_first(way, step + 1, sub, False).start()
-
-    for d in (4, 2, -2):
+            around(way, 1, o, False).start()
+
+    def round_step(step, o):
+        for way in ways(step, o):
+            around(way, step, o, True).wait_recv()
+            if step < SIDE // 2 and way in ways(step + 1, o):
+                around(way, step + 1, o, False).start()
+
+    for d in (2, -2, 4):
         alike(d, False).start()
+    round_begin(0)
+    query_steps((2, 0), (2, 1))
+    round_step(1, 0)
+    for d in (2, -2):
+        alike(d, True).wait_recv()
+        round_begin(-d)
+    query_steps((3, 0))
+    alike(4, True).wait_recv()
+    round_begin(4)
+    round_step(2, 0)
+    round_step(1, 2)
+    round_step(1, -2)
+    query_steps((3, 1))
+    round_step(1, 4)
+    round_step(3, 0)
+    round_step(2, 2)
+    round_step(2, -2)
+    query_steps((4, 0), (4, 1))
+    round_step(2, 4)
+    round_step(4, 0)
+    round_step(3, 2)
+    round_step(3, -2)
     behind = [
         copy(("prior", "k"), kt.at[0], kt.at[1], span_next),
         copy(("prior", "v"), vv.at[0], vv.at[1], span_next),
     ]
     for one in behind:
         one.start()
-    query_steps((2, 1), (3, 0), (3, 1))
-    for d in (2, -2, 4):
-        alike(d, True).wait_recv()
-    for step in query.steps[:4]:
-        round_first(*step, False).start()
-    query_steps((4, 0), (4, 1))
-    round_step(1, 0)
     per_row(query.from_sibling)
 
     qraw[:, :left_cols] = project_all(wq0)
-    round_step(1, 1)
+    round_step(3, 4)
     qraw[:, left_cols:] = project_all(wq1)
-    round_step(2, 0)
 
     def rotate_head(g):
         columns = pl.ds(pl.multiple_of(g * width, width), width)
@@ -324,9 +373,9 @@
         qf[g] = (raw * fixed[0:1] + swapped * fixed[1:2]).astype(BF16)
 
     pl.loop(0, 4)(rotate_head)
-    round_step(2, 1)
+    round_step(4, 2)
+    round_step(4, -2)
     pl.loop(4, group)(rotate_head)
-    round_step(3, 0)
     for one in behind:
         one.wait_recv()
 
@@ -345,10 +394,7 @@
         )
 
     pl.loop(0, 1)(close_part)
-    round_step(3, 1)
-    pl.loop(1, 2)(close_part)
-    round_step(4, 0)
-    round_step(4, 1)
+    round_step(4, 4)
 
     def place_of(span):
         across, down = span % SIDE, span // SIDE
@@ -357,28 +403,33 @@
     for one in list_sends:
         one.wait_recv()
     each = slots // 2
+    trades = {}
+    for which in range(2):
+        for side, d in ((0, 1), (1, -1)):
+            for e in range(each):
+                one, two = place_of(lists[side, 0, side * each + e])
+                chosen[side, which, e] = pool[one, two // 2, which]
+            src, dst = chosen.at[side, which], got.at[side, which]
+            trades[side, which] = copy(("trade", d, which), src, dst, along2(d))
+            trades[side, which].start()
+    pl.loop(1, group)(close_part)
+
+    def listed(e, which):
+        one, two = place_of(vertical[0, 0, e])
+        traded = got[e // each, which, e % each]
+        return jnp.where(two % 2 == pos2 % 2, pool[one, two // 2, which], traded)
+
     for side in range(2):
-        for e in range(each):
-            one, two = place_of(lists[side, 0, side * each + e])
-            chosen[side, e] = pool[one, two // 2]
-    trades = [copy(("trade", d), chosen.at[i], got.at[i], along2(d)) for i, d in ((0, 1), (1, -1))]
-    for one in trades:
-        one.start()
-    pl.loop(2, group)(close_part)
-    for one in trades:
-        one.wait_recv()
-
+        trades[side, 0].wait_recv()
     for e in range(slots):
-        one, two = place_of(vertical[0, 0, e])
-        same = two % 2 == pos2 % 2
-        block = jnp.where(same, pool[one, two // 2], got[e // each, e % each])
-        kft[:, e * BLOCK : (e + 1) * BLOCK] = block[0]
-        vft[e * BLOCK : (e + 1) * BLOCK] = block[1]
+        kft[:, e * BLOCK : (e + 1) * BLOCK] = listed(e, 0)
     place = lax.broadcasted_iota(jnp.int32, (1, slots * BLOCK), 1)
     bias_far = jnp.where(place < vcount[0, 0] * BLOCK, 0.0, MASKED)
 
-    def far_part(g):
-        scores = jnp.dot(qf[g], kft[...], preferred_element_type=F32) * score_scale + bias_far
+    def far_scores(g):
+        return jnp.dot(qf[g], kft[...], preferred_element_type=F32) * score_scale + bias_far
+
+    def far_part(g, scores):
         before = top1[g][:, :1]
         highest = jnp.maximum(before, jnp.max(scores, axis=1, keepdims=True))
         weights = jnp.exp2(scores - highest)
@@ -387,22 +438,36 @@
         combined = acc1[g] * fade + jnp.dot(
             weights.astype(BF16), vft[...], preferred_element_type=F32
         )
-        columns = pl.ds(pl.multiple_of(g * width, width), width)
+        columns = pl.ds(g * width, width)
         out[:, columns] = (combined / total).astype(BF16)
-
-    pl.loop(0, group)(far_part)
+        pltpu.make_async_copy(out.at[:, columns], out_hbm.at[:, columns], osem.at[g]).start()
+
+    scores = far_scores(0)
+    for side in range(2):
+        trades[side, 1].wait_recv()
+    for e in range(slots):
+        vft[e * BLOCK : (e + 1) * BLOCK] = listed(e, 1)
+    for g in range(group):
+        far_part(g, scores)
+        if g + 1 < group:
+            scores = far_scores(g + 1)
 
     for way, sub in ((1, 0), (-1, 1), (1, 1), (-1, 0)):
         feature(way, sub, False, False).wait_send()
     for way, sub in ((1, 0), (-1, 1)):
         feature(way, sub, True, False).wait_send()
-    for one in behind + trades + list_sends:
+    for one in behind + list(trades.values()) + list_sends:
         one.wait_send()
     for d in (4, 2, -2):
         alike(d, False).wait_send()
-    for step in query.steps:
-        round_first(*step, False).wait_send()
+    for o in offsets:
+        for step in (1, 2, 3, 4):
+            for way in ways(step, o):
+                around(way, step, o, False).wait_send()
     per_row(lambda rr: [one.finish(rr) for one in (kv, query)] and None)
+    for g in range(group):
+        columns = pl.ds(g * width, width)
+        pltpu.make_async_copy(out.at[:, columns], out_hbm.at[:, columns], osem.at[g]).wait()
 
 
 def on_device(
@@ -419,22 +484,28 @@
     moving, fixed = rope_tables(tokens, width)
     hbm = pl.BlockSpec(memory_space=pl.ANY)
     vmem = pl.BlockSpec(memory_space=pltpu.VMEM)
-    smem = pl.BlockSpec(memory_space=pltpu.SMEM)
     copies = 160
     return pl.pallas_call(
         kernel,
         out_shape=jax.ShapeDtypeStruct((tokens, columns), BF16),
-        in_specs=[hbm] * 4 + [vmem] * 3 + [smem] * 5 + [hbm] + [vmem] * 2,
-        out_specs=vmem,
+        in_specs=[hbm] * 10 + [vmem] * 4,
+        out_specs=hbm,
         scratch_shapes=[
+            pltpu.VMEM((tokens, columns), BF16),
+            pltpu.VMEM(moving.shape, F32),
+            pltpu.SMEM(published.shape, jnp.int32),
+            pltpu.SMEM(vertical.shape, jnp.int32),
+            pltpu.SMEM(vcount.shape, jnp.int32),
+            pltpu.SMEM(slash_offsets.shape, jnp.int32),
+            pltpu.SMEM(scount.shape, jnp.int32),
             pltpu.VMEM((heads, tokens, part), BF16),
             pltpu.VMEM((SIDE, SIDE, depth, width), BF16),
             pltpu.VMEM((SIDE, SIDE, depth, width), BF16),
             pltpu.VMEM((SIDE, SIDE, depth, left), BF16),
             pltpu.VMEM((SIDE, SIDE, depth, columns - left), BF16),
             pltpu.VMEM((SIDE, SIDE // 2, 2, BLOCK, width), BF16),
-            pltpu.VMEM((2, slots // 2, 2, BLOCK, width), BF16),
-            pltpu.VMEM((2, slots // 2, 2, BLOCK, width), BF16),
+            pltpu.VMEM((2, 2, slots // 2, BLOCK, width), BF16),
+            pltpu.VMEM((2, 2, slots // 2, BLOCK, width), BF16),
             pltpu.SMEM((2, 1, slots), jnp.int32),
             pltpu.VMEM((2, width, tokens), BF16),
             pltpu.VMEM((2, tokens, width), BF16),
@@ -451,7 +522,8 @@
             pltpu.VMEM((tokens, tokens), F32),
             pltpu.SemaphoreType.DMA((copies,)),
             pltpu.SemaphoreType.DMA((copies,)),
-            pltpu.SemaphoreType.DMA((3,)),
+            pltpu.SemaphoreType.DMA((9,)),
+            pltpu.SemaphoreType.DMA((group,)),
         ],
         compiler_params=pltpu.CompilerParams(
             collective_id=0, has_side_effects=True, vmem_limit_bytes=56 * 1024 * 1024
@@ -460,11 +532,9 @@
             flops=4 * 10**9, bytes_accessed=10**7, transcendentals=3 * 10**6
         ),
     )(
-        hidden_states, key_weight_matrix, value_weight_matrix, w_query,
-        bias_query, bias_key.reshape(1, width),
-        value_bias_vector.reshape(1, width),
+        hidden_states, key_weight_matrix, value_weight_matrix, w_query, jnp.asarray(moving),
         published, vertical, vcount, slash_offsets, scount,
-        vertical[0], jnp.asarray(moving), jnp.asarray(fixed),
+        bias_query, bias_key, value_bias_vector, jnp.asarray(fixed),
     )
 
 

time: 91.6 us -> 83.5 us (0.912)
  Pallas kernels: 87.1 us -> 79.2 us
    pallas_call x1, Pallas kernels: 87.1 us -> 79.2 us  [on_device(): pl.pallas_call(kernel, out_shape=jax.ShapeDtypeStruct((tokens, columns),...]
where the time goes in v3:
time: 83.5 us; the launch traced here: 83 us
  Pallas kernels  79.2 us (95%)
  between operations  1.95 us (2%)
  local copies, waits for them, and re-layouts  1.82 us (2%)
    pallas_call x1, Pallas kernels, on_device(): pl.pallas_call(kernel, out_shape=jax.ShapeDtypeStruct((tokens, columns),...  79.2 us
    unnamed x1, local copies, waits for them, and re-layouts  1.82 us

profile of v3, /device:TPU:6, one launch (start us, length us, event | category | flops | bytes accessed | tf_op | source)
XLA Modules:
  0.0 83.0 jit_solution(11485222269687256723)
XLA Ops:
  1.9 79.2 %shard_map.136 = bf16[256,896]{1,0:T(8,128)(2,1)} custom-call(bf16[256,896]{1,0:T(8,128)(2,1)} %hid.1, bf16[56,128]{1,0:T(8,128)(2,1)} %wk.1, bf16[56,128]{1,0:T(8,128)(2,1)} %wv.1, bf16[56,896]{1,0:T(8,128)(2,1)} %wq.1, f32[4,256,128]{2,1,0:T(8,128)} %constant.4.clone.moving_hbm, s32[1,1]{1,0:T(1,128)S(6)} %copy.16.published_hbm, s32[1,1,8]{2,1,0:T(1,128)} %vertical_hbm.1, ...), custom_call_target="tpu_custom_call" | custom-call | flops 4000000000 | bytes 10000000 | tf_op jit(solution)/shard_map/pallas_call | solution.py:488
  81.2 1.8 %copy.19 = bf16[256,896]{1,0:T(8,128)(2,1)} copy(bf16[256,896]{1,0:T(8,128)(2,1)} %shard_map.136) | data formatting | bytes 917504

commit v4 on v3

--- a/solution.py
+++ b/solution.py
@@ -12,6 +12,7 @@
 SIDE = 8
 MASKED = -1e30
 FIRST_ORDER = (4, 3, -3, 2, -2, 1, -1)
+REACH = 2
 LOG2E = 1.4426950408889634
 BF16, F32 = jnp.bfloat16, jnp.float32
 
@@ -41,8 +42,8 @@
 def kernel(
     hid, wk, wv, wq, moving_hbm, published_hbm, vertical_hbm, vcount_hbm, slash_hbm, scount_hbm,
     bq, bk, bv, fixed,
-    out_hbm,
-    out, moving, published, vertical, vcount, slash, scount, hbuf, wkb, wvb, wq0, wq1, pool, chosen, got, lists, kt, vv, qraw, ql, qn, qf, kft, vft,
+    out,
+    moving, published, vertical, vcount, slash, scount, hbuf, wkb, wvb, wq0, wq1, pool, chosen, got, lists, kt, vv, qraw, ql, qn, qf, kft, vft,
     top1, sum1, acc1, bias_local, bias_near,
     send, recv, lsem, osem,
 ):
@@ -94,20 +95,25 @@
         def __init__(self, name, bufs):
             self.name, self.bufs = name, bufs
 
-        def slot(self, rr, i):
+        def slot(self, rr, away):
+            i = (away + REACH + SIDE) % SIDE
             return self.bufs[rr].at[y, i] if rr == 0 else self.bufs[rr].at[i, z]
 
         def unit(self, rr, away, sub=None):
             i = (pos2 + away + SIDE) % SIDE
             if sub is None:
                 return self.bufs[rr].at[i] if rr == 0 else self.bufs[rr].at[:, i]
-            cut = pl.ds(sub * (SIDE // 2), SIDE // 2)
+            cut = pl.ds(sub * (2 * REACH + 1), (2 * REACH + 1, SIDE - 2 * REACH - 1)[sub])
             return self.bufs[rr].at[i, cut] if rr == 0 else self.bufs[rr].at[cut, i]
 
         def first(self, rr, move, arriving):
             d, away = move
-            ref = self.slot(rr, (pos1 + (away - d if arriving else away) + SIDE) % SIDE)
-            return copy((self.name, "first", move), ref, ref, along1(d))
+            return copy(
+                (self.name, "first", move),
+                self.slot(rr, away - d if arriving else away),
+                self.slot(rr, away - d),
+                along1(d),
+            )
 
         def first_begin(self, rr, moves):
             for move in moves:
@@ -144,17 +150,21 @@
                 self.to_sibling(rr, move[1] - move[0], move[2]).wait_send()
 
     kv, query = Weights("kv", (wkb, wvb)), Weights("q", (wq0, wq1))
-    kv.near, kv.far = [(d, 0) for d in FIRST_ORDER], []
+    kv.near = [(2, 0), (-2, 0), (1, 0), (-1, 0)]
+    kv.far = [(4, 0), (3, 0), (-3, 0)]
     query.near, query.far = [(2, 0), (-2, 0), (1, 0), (-1, 0)], [(2, -2), (1, -2), (-1, 2)]
-    kv.one = [(1, 0, None), (-1, 0, None), (2, 0, None), (-2, 0, None)]
-    kv.two = [(1, -2, None), (-1, 2, None), (2, -2, 0), (-2, 2, 1)]
-    kv.moves = kv.one + kv.two
+    kv.one = [[(d, 0, sub) for d in (2, -2, 1, -1)] for sub in (0, 1)]
+    kv.two = [
+        [(1, -2, 0), (-1, 2, 0), (-2, 2, 0)],
+        [(1, -2, 1), (-1, 2, 1), (2, -2, 1)],
+    ]
+    kv.moves = kv.one[0] + kv.one[1] + kv.two[0] + kv.two[1]
 
     def query_move(way, step, sub):
         return (way, -way * (step - 1), sub)
 
     query.steps = [(w, s, b) for s in (1, 2, 3) for b in (0, 1) for w in (1, -1)]
-    query.steps += [(1, SIDE // 2, 0), (-1, SIDE // 2, 1)]
+    query.steps += [(-1, SIDE // 2, 0), (1, SIDE // 2, 1)]
     query.moves = [query_move(*step) for step in query.steps]
 
     def query_begin(rr, sub):
@@ -191,8 +201,8 @@
     def own_weights(rr):
         columns = pl.ds(0, left_cols) if rr == 0 else pl.ds(left_cols, wq.shape[1] - left_cols)
         return (
-            pltpu.make_async_copy((wk, wv)[rr], (wkb, wvb)[rr].at[y, z], lsem.at[1]),
-            pltpu.make_async_copy(wq.at[:, columns], (wq0, wq1)[rr].at[y, z], lsem.at[2]),
+            pltpu.make_async_copy((wk, wv)[rr], kv.slot(rr, 0), lsem.at[1]),
+            pltpu.make_async_copy(wq.at[:, columns], query.slot(rr, 0), lsem.at[2]),
         )
 
     per_row(lambda rr: [one.start() for one in own_weights(rr)] and None)
@@ -207,7 +217,7 @@
     def weights_begin(rr):
         first, second = own_weights(rr)
         first.wait()
-        kv.first_begin(rr, kv.near)
+        kv.first_begin(rr, kv.near + kv.far)
         second.wait()
         query.first_begin(rr, query.near)
 
@@ -242,13 +252,23 @@
         near = jnp.where(back == offset, 0.0, near)
     bias_near[...] = near
 
+    def kv_send(rr, moves):
+        for move in moves:
+            kv.second(rr, move, False).start()
+
+    def kv_take(rr, moves):
+        for move in moves:
+            kv.second(rr, move, True).wait_recv()
+
     def kv_first(rr):
         kv.first_end(rr, kv.near)
-        for move in kv.one:
-            kv.second(rr, move, False).start()
-        kv.to_sibling(rr, 0).start()
+        kv_send(rr, kv.one[0])
+        kv.first_end(rr, kv.far)
+        kv_send(rr, kv.one[1])
         query.first_end(rr, query.near)
         query.first_begin(rr, query.far)
+        query_begin(rr, 0)
+        kv.to_sibling(rr, 0).start()
 
     per_row(kv_first)
     for way, sub in ((1, 0), (-1, 1)):
@@ -256,20 +276,19 @@
         feature(way, sub, True, False).start()
 
     def spread(rr):
+        for sub in (0, 1):
+            kv_take(rr, kv.one[sub])
+            kv_send(rr, kv.two[sub])
+        for move in kv.one[0] + kv.one[1]:
+            kv.pass_on(rr, move)
         query.first_end(rr, query.far)
-        query_begin(rr, 0)
-        for move in kv.one:
-            kv.second(rr, move, True).wait_recv()
-        for move in kv.two:
-            kv.second(rr, move, False).start()
         query_begin(rr, 1)
-        for move in kv.one:
-            kv.pass_on(rr, move)
         query.to_sibling(rr, 0).start()
         query_step(rr, 1, 0)
-        for move in kv.two:
-            kv.second(rr, move, True).wait_recv()
-            kv.pass_on(rr, move)
+        for sub in (0, 1):
+            kv_take(rr, kv.two[sub])
+            for move in kv.two[sub]:
+                kv.pass_on(rr, move)
         query_step(rr, 1, 1)
         kv.from_sibling(rr)
 
@@ -279,9 +298,19 @@
     for way, sub in ((1, 0), (-1, 1)):
         feature(way, sub, True, True).wait_recv()
 
+    def gathered(h, rr, one):
+        def rank(i, pos):
+            return (i - pos + REACH + SIDE) % SIDE
+
+        down, across = [2 * h, 2 * h + 1], range(SIDE)
+        if rr == 0:
+            across = [rank(i, z) for i in across]
+        else:
+            down = [rank(i, y) for i in down]
+        return jnp.concatenate([one[i, j] for i in down for j in across], axis=0)
+
     def project(h, *weights):
-        parts = [one.at[pl.ds(2 * h, 2)][...] for one in weights]
-        block = jnp.concatenate([one.reshape(part, one.shape[-1]) for one in parts], axis=1)
+        block = jnp.concatenate([gathered(h, rr, one) for rr, one in weights], axis=1)
         return jnp.dot(hbuf[h], block, preferred_element_type=F32)
 
     def project_all(*weights):
@@ -293,7 +322,7 @@
     def query_steps(*steps):
         per_row(lambda rr: [query_step(rr, *one) for one in steps] and None)
 
-    both = project_all(wkb, wvb)
+    both = project_all((0, wkb), (1, wvb))
     keys = rotate(both[:, :width] + bk[...][None, :], moving[0], moving[1]).astype(BF16)
     kt[0] = keys.T
     vv[0] = (both[:, width:] + bv[...][None, :]).astype(BF16)
@@ -336,6 +365,11 @@
     for d in (2, -2):
         alike(d, True).wait_recv()
         round_begin(-d)
+    for way, sub in ((1, 0), (-1, 1), (1, 1), (-1, 0)):
+        feature(way, sub, False, False).wait_send()
+    for way, sub in ((1, 0), (-1, 1)):
+        feature(way, sub, True, False).wait_send()
+    per_row(kv.finish)
     query_steps((3, 0))
     alike(4, True).wait_recv()
     round_begin(4)
@@ -360,9 +394,9 @@
         one.start()
     per_row(query.from_sibling)
 
-    qraw[:, :left_cols] = project_all(wq0)
+    qraw[:, :left_cols] = project_all((0, wq0))
     round_step(3, 4)
-    qraw[:, left_cols:] = project_all(wq1)
+    qraw[:, left_cols:] = project_all((1, wq1))
 
     def rotate_head(g):
         columns = pl.ds(pl.multiple_of(g * width, width), width)
@@ -419,6 +453,15 @@
         traded = got[e // each, which, e % each]
         return jnp.where(two % 2 == pos2 % 2, pool[one, two // 2, which], traded)
 
+    per_row(query.finish)
+    for d in (4, 2, -2):
+        alike(d, False).wait_send()
+    for o in offsets:
+        for step in (1, 2, 3, 4):
+            for way in ways(step, o):
+                around(way, step, o, False).wait_send()
+    for one in behind + list_sends:
+        one.wait_send()
     for side in range(2):
         trades[side, 0].wait_recv()
     for e in range(slots):
@@ -440,7 +483,6 @@
         )
         columns = pl.ds(g * width, width)
         out[:, columns] = (combined / total).astype(BF16)
-        pltpu.make_async_copy(out.at[:, columns], out_hbm.at[:, columns], osem.at[g]).start()
 
     scores = far_scores(0)
     for side in range(2):
@@ -452,22 +494,8 @@
         if g + 1 < group:
             scores = far_scores(g + 1)
 
-    for way, sub in ((1, 0), (-1, 1), (1, 1), (-1, 0)):
-        feature(way, sub, False, False).wait_send()
-    for way, sub in ((1, 0), (-1, 1)):
-        feature(way, sub, True, False).wait_send()
-    for one in behind + list(trades.values()) + list_sends:
+    for one in trades.values():
         one.wait_send()
-    for d in (4, 2, -2):
-        alike(d, False).wait_send()
-    for o in offsets:
-        for step in (1, 2, 3, 4):
-            for way in ways(step, o):
-                around(way, step, o, False).wait_send()
-    per_row(lambda rr: [one.finish(rr) for one in (kv, query)] and None)
-    for g in range(group):
-        columns = pl.ds(g * width, width)
-        pltpu.make_async_copy(out.at[:, columns], out_hbm.at[:, columns], osem.at[g]).wait()
 
 
 def on_device(
@@ -487,11 +515,10 @@
     copies = 160
     return pl.pallas_call(
         kernel,
-        out_shape=jax.ShapeDtypeStruct((tokens, columns), BF16),
+        out_shape=pltpu.VMEM((tokens, columns), BF16),
         in_specs=[hbm] * 10 + [vmem] * 4,
-        out_specs=hbm,
+        out_specs=pl.BlockSpec(memory_space=pltpu.VMEM),
         scratch_shapes=[
-            pltpu.VMEM((tokens, columns), BF16),
             pltpu.VMEM(moving.shape, F32),
             pltpu.SMEM(published.shape, jnp.int32),
             pltpu.SMEM(vertical.shape, jnp.int32),

time: 83.5 us -> 78.1 us (0.935)
  Pallas kernels: 79.2 us -> 75.2 us
  local copies, waits for them, and re-layouts: 1.82 us -> 0.77 us
    pallas_call x1, Pallas kernels: 79.2 us -> 75.2 us  [on_device(): pl.pallas_call(kernel, out_shape=pltpu.VMEM((tokens, columns), BF16), in_...]
    unnamed x1, local copies, waits for them, and re-layouts: 1.82 us -> 0.77 us
where the time goes in v4:
time: 78.1 us; the launch traced here: 77.9 us
  Pallas kernels  75.2 us (96%)
  between operations  1.95 us (2%)
    pallas_call x1, Pallas kernels, on_device(): pl.pallas_call(kernel, out_shape=pltpu.VMEM((tokens, columns), BF16), in_...  75.2 us

profile of v4, /device:TPU:6, one launch (start us, length us, event | category | flops | bytes accessed | tf_op | source)
XLA Modules:
  0.0 77.9 jit_solution(10404260395925513983)
XLA Ops:
  1.9 75.2 %shard_map.136 = bf16[256,896]{1,0:T(8,128)(2,1)S(1)} custom-call(bf16[256,896]{1,0:T(8,128)(2,1)} %hid.1, bf16[56,128]{1,0:T(8,128)(2,1)} %wk.1, bf16[56,128]{1,0:T(8,128)(2,1)} %wv.1, bf16[56,896]{1,0:T(8,128)(2,1)} %wq.1, f32[4,256,128]{2,1,0:T(8,128)} %constant.4.clone.moving_hbm, s32[1,1]{1,0:T(1,128)S(6)} %copy.17.published_hbm, ...), custom_call_target="tpu_custom_call" | custom-call | flops 4000000000 | bytes 10000000 | tf_op jit(solution)/shard_map/pallas_call | solution.py:516
  77.1 0.8 copy.16

commit v5 on v4

--- a/solution.py
+++ b/solution.py
@@ -41,9 +41,9 @@
 
 def kernel(
     hid, wk, wv, wq, moving_hbm, published_hbm, vertical_hbm, vcount_hbm, slash_hbm, scount_hbm,
-    bq, bk, bv, fixed,
+    bq_hbm, bk_hbm, bv_hbm, fixed_hbm,
     out,
-    moving, published, vertical, vcount, slash, scount, hbuf, wkb, wvb, wq0, wq1, pool, chosen, got, lists, kt, vv, qraw, ql, qn, qf, kft, vft,
+    bq, bk, bv, fixed, moving, published, vertical, vcount, slash, scount, hbuf, wkb, wvb, wq0, wq1, pool, chosen, got, lists, kt, vv, qraw, ql, qn, qf, kft, vft,
     top1, sum1, acc1, bias_local, bias_near,
     send, recv, lsem, osem,
 ):
@@ -178,6 +178,12 @@
                 if (way, step + 1, sub) in query.steps:
                     query.second(rr, query_move(way, step + 1, sub), False).start()
                 query.pass_on(rr, query_move(way, step, sub))
+
+    barrier = pltpu.get_barrier_semaphore()
+    partners = [along1(d) for d in FIRST_ORDER] + [along2(d) for d in (1, -1, 2, -2, 4)]
+    partners += [sibling, x_right, x_left, span_next, span_prior]
+    for device in partners:
+        pl.semaphore_signal(barrier, inc=1, device_id=device, device_id_type=pl.DeviceIdType.MESH)
 
     own_hidden = pltpu.make_async_copy(hid, hbuf.at[x], lsem.at[0])
     own_hidden.start()
@@ -192,6 +198,10 @@
                 (vcount_hbm, vcount),
                 (slash_hbm, slash),
                 (scount_hbm, scount),
+                (bq_hbm, bq),
+                (bk_hbm, bk),
+                (bv_hbm, bv),
+                (fixed_hbm, fixed),
             )
         )
     ]
@@ -207,11 +217,6 @@
 
     per_row(lambda rr: [one.start() for one in own_weights(rr)] and None)
 
-    barrier = pltpu.get_barrier_semaphore()
-    partners = [along1(d) for d in FIRST_ORDER] + [along2(d) for d in (1, -1, 2, -2, 4)]
-    partners += [sibling, x_right, x_left, span_next, span_prior]
-    for device in partners:
-        pl.semaphore_signal(barrier, inc=1, device_id=device, device_id_type=pl.DeviceIdType.MESH)
     pl.semaphore_wait(barrier, len(partners))
 
     def weights_begin(rr):
@@ -345,7 +350,7 @@
         return copy(("round", way, step, o), ref, ref, along1(way))
 
     def ways(step, o):
-        return (1, -1) if step < SIDE // 2 else (1,) if o in (0, 2) else (-1,)
+        return (1, -1) if step < SIDE // 2 else (-1,)
 
     def round_begin(o):
         for way in (1, -1):
@@ -370,33 +375,29 @@
     for way, sub in ((1, 0), (-1, 1)):
         feature(way, sub, True, False).wait_send()
     per_row(kv.finish)
-    query_steps((3, 0))
     alike(4, True).wait_recv()
     round_begin(4)
     round_step(2, 0)
     round_step(1, 2)
     round_step(1, -2)
+    query_steps((3, 0))
+    round_step(1, 4)
     query_steps((3, 1))
-    round_step(1, 4)
-    round_step(3, 0)
-    round_step(2, 2)
-    round_step(2, -2)
-    query_steps((4, 0), (4, 1))
-    round_step(2, 4)
-    round_step(4, 0)
-    round_step(3, 2)
-    round_step(3, -2)
     behind = [
         copy(("prior", "k"), kt.at[0], kt.at[1], span_next),
         copy(("prior", "v"), vv.at[0], vv.at[1], span_next),
     ]
     for one in behind:
         one.start()
-    per_row(query.from_sibling)
-
-    qraw[:, :left_cols] = project_all((0, wq0))
-    round_step(3, 4)
-    qraw[:, left_cols:] = project_all((1, wq1))
+    round_step(3, 0)
+    round_step(2, 2)
+    round_step(2, -2)
+
+    def last_steps(rr):
+        for sub in (0, 1):
+            query_step(rr, SIDE // 2, sub)
+
+    per_row(lambda rr: query.from_sibling(rr) if rr else last_steps(rr))
 
     def rotate_head(g):
         columns = pl.ds(pl.multiple_of(g * width, width), width)
@@ -406,10 +407,19 @@
         qn[g] = (raw * moving[2] + swapped * moving[3]).astype(BF16)
         qf[g] = (raw * fixed[0:1] + swapped * fixed[1:2]).astype(BF16)
 
-    pl.loop(0, 4)(rotate_head)
+    left_heads = left_cols // width
+    qraw[:, :left_cols] = project_all((0, wq0))
+    round_step(2, 4)
+    round_step(4, 0)
+    round_step(3, 2)
+    round_step(3, -2)
+    pl.loop(0, left_heads)(rotate_head)
+    per_row(lambda rr: last_steps(rr) if rr else query.from_sibling(rr))
+    round_step(3, 4)
+    qraw[:, left_cols:] = project_all((1, wq1))
     round_step(4, 2)
     round_step(4, -2)
-    pl.loop(4, group)(rotate_head)
+    pl.loop(left_heads, group)(rotate_head)
     for one in behind:
         one.wait_recv()
 
@@ -490,9 +500,9 @@
     for e in range(slots):
         vft[e * BLOCK : (e + 1) * BLOCK] = listed(e, 1)
     for g in range(group):
+        following = far_scores(g + 1) if g + 1 < group else None
         far_part(g, scores)
-        if g + 1 < group:
-            scores = far_scores(g + 1)
+        scores = following
 
     for one in trades.values():
         one.wait_send()
@@ -511,14 +521,17 @@
     left = (group // 2) * width
     moving, fixed = rope_tables(tokens, width)
     hbm = pl.BlockSpec(memory_space=pl.ANY)
-    vmem = pl.BlockSpec(memory_space=pltpu.VMEM)
     copies = 160
     return pl.pallas_call(
         kernel,
         out_shape=pltpu.VMEM((tokens, columns), BF16),
-        in_specs=[hbm] * 10 + [vmem] * 4,
+        in_specs=[hbm] * 14,
         out_specs=pl.BlockSpec(memory_space=pltpu.VMEM),
         scratch_shapes=[
+            pltpu.VMEM(bias_query.shape, F32),
+            pltpu.VMEM(bias_key.shape, F32),
+            pltpu.VMEM(value_bias_vector.shape, F32),
+            pltpu.VMEM(fixed.shape, F32),
             pltpu.VMEM(moving.shape, F32),
             pltpu.SMEM(published.shape, jnp.int32),
             pltpu.SMEM(vertical.shape, jnp.int32),
@@ -549,7 +562,7 @@
             pltpu.VMEM((tokens, tokens), F32),
             pltpu.SemaphoreType.DMA((copies,)),
             pltpu.SemaphoreType.DMA((copies,)),
-            pltpu.SemaphoreType.DMA((9,)),
+            pltpu.SemaphoreType.DMA((13,)),
             pltpu.SemaphoreType.DMA((group,)),
         ],
         compiler_params=pltpu.CompilerParams(

time: 78.1 us -> 77.5 us (level)
  Pallas kernels: 75.2 us -> 73.9 us
    pallas_call x1, Pallas kernels: 75.2 us -> 73.9 us  [on_device(): pl.pallas_call(kernel, out_shape=pltpu.VMEM((tokens, columns), BF16), in_...]
where the time goes in v5:
time: 77.5 us; the launch traced here: 76.6 us
  Pallas kernels  73.9 us (95%)
  between operations  1.95 us (3%)
    pallas_call x1, Pallas kernels, on_device(): pl.pallas_call(kernel, out_shape=pltpu.VMEM((tokens, columns), BF16), in_...  73.9 us

profile of v5, /device:TPU:6, one launch (start us, length us, event | category | flops | bytes accessed | tf_op | source)
XLA Modules:
  0.0 76.6 jit_solution(16799639276529911644)
XLA Ops:
  1.9 73.9 %shard_map.136 = bf16[256,896]{1,0:T(8,128)(2,1)S(1)} custom-call(bf16[256,896]{1,0:T(8,128)(2,1)} %hid.1, bf16[56,128]{1,0:T(8,128)(2,1)} %wk.1, bf16[56,128]{1,0:T(8,128)(2,1)} %wv.1, bf16[56,896]{1,0:T(8,128)(2,1)} %wq.1, f32[4,256,128]{2,1,0:T(8,128)} %constant.4.clone.moving_hbm, s32[1,1]{1,0:T(1,128)S(6)} %copy.17.published_hbm, ...), custom_call_target="tpu_custom_call" | custom-call | flops 4000000000 | bytes 10000000 | tf_op jit(solution)/shard_map/pallas_call | solution.py:525
  75.8 0.8 %copy.16 = bf16[256,896]{1,0:T(8,128)(2,1)} copy(bf16[256,896]{1,0:T(8,128)(2,1)S(1)} %shard_map.136) | data formatting | bytes 917504

commit v6 on v5

--- a/solution.py
+++ b/solution.py
@@ -419,7 +419,7 @@
     qraw[:, left_cols:] = project_all((1, wq1))
     round_step(4, 2)
     round_step(4, -2)
-    pl.loop(left_heads, group)(rotate_head)
+    pl.loop(left_heads, group, unroll=True)(rotate_head)
     for one in behind:
         one.wait_recv()
 
@@ -456,7 +456,7 @@
             src, dst = chosen.at[side, which], got.at[side, which]
             trades[side, which] = copy(("trade", d, which), src, dst, along2(d))
             trades[side, which].start()
-    pl.loop(1, group)(close_part)
+    pl.loop(1, group, unroll=True)(close_part)
 
     def listed(e, which):
         one, two = place_of(vertical[0, 0, e])

time: 77.5 us -> 77.5 us (level)
  no operation moved by 1% of the time
where the time goes in v6:
time: 77.5 us; the launch traced here: 76.6 us
  Pallas kernels  73.9 us (95%)
  between operations  1.95 us (3%)
    pallas_call x1, Pallas kernels, on_device(): pl.pallas_call(kernel, out_shape=pltpu.VMEM((tokens, columns), BF16), in_...  73.9 us

profile of v6, /device:TPU:6, one launch (start us, length us, event | category | flops | bytes accessed | tf_op | source)
XLA Modules:
  0.0 76.6 jit_solution(618396632553131413)
XLA Ops:
  1.9 73.9 %shard_map.136 = bf16[256,896]{1,0:T(8,128)(2,1)S(1)} custom-call(bf16[256,896]{1,0:T(8,128)(2,1)} %hid.1, bf16[56,128]{1,0:T(8,128)(2,1)} %wk.1, bf16[56,128]{1,0:T(8,128)(2,1)} %wv.1, bf16[56,896]{1,0:T(8,128)(2,1)} %wq.1, f32[4,256,128]{2,1,0:T(8,128)} %constant.4.clone.moving_hbm, s32[1,1]{1,0:T(1,128)S(6)} %copy.17.published_hbm, ...), custom_call_target="tpu_custom_call" | custom-call | flops 4000000000 | bytes 10000000 | tf_op jit(solution)/shard_map/pallas_call | solution.py:525
  75.8 0.8 %copy.16 = bf16[256,896]{1,0:T(8,128)(2,1)} copy(bf16[256,896]{1,0:T(8,128)(2,1)S(1)} %shard_map.136) | data formatting | bytes 917504
